TPU v7x, 32 devices: a whole 2x2x4 slice. The times are simulated.
32 devices in a mesh: expert: 4 (over y, core), dp: 8 (over z, x).
Axes of the slice: x: 2, y: 2, z: 4, core: 2. Of those that a mesh axis runs over, the one named last changes fastest.
Arguments:
- tokens: bfloat16 [4096, 3584], P(('expert', 'dp')), may hold values from -6 to 6
- grad_out: bfloat16 [4096, 3584], P(('expert', 'dp')), may hold values from -4 to 4
- route_weights: float32 [4096, 8], P(('expert', 'dp')), may hold values from 0.05 to 0.5
- expert_ids: int32 [4096, 8], P(('expert', 'dp')), may hold values from 0 to 255, all different within a row; in each aligned block of 128 rows (0 to 127, 128 to 255, ...) at most 5 rows name the same one
- swap_code: int32 [4], replicated, may hold values from 0 to 3, as said below
- w_in: bfloat16 [4, 2, 2048, 3584], P('expert', None, 'dp'), may hold values from -0.09375 to 0.09375
- w_down: bfloat16 [4, 2048, 3584], P('expert', 'dp'), may hold values from -0.125 to 0.125
- moment1: float32 [4, 2048, 3584], P('expert', 'dp'), may hold values from -6 to 6
- moment2: float32 [4, 2048, 3584], P('expert', 'dp'), may hold values from 0.05 to 1
Outputs:
- new_down: bfloat16 [4, 2048, 3584], P('expert', 'dp')
- new_moment1: float32 [4, 2048, 3584], P('expert', 'dp')
- new_moment2: float32 [4, 2048, 3584], P('expert', 'dp')
- grad_in: bfloat16 [4, 2, 2048, 3584], P('expert', None, 'dp')
Inputs may be any that keep to these rules, and one draw needn't show every extreme that they name: `expert_ids`: each row names 8 different experts; in the rows of one device no expert is named more than 5 times. `swap_code`: entry 0 has all of its 2 low bits set.
All inputs are finite; a program needn't handle non-finite values.
Results may differ from a plain program's by a relative error of at most 0.0057.
Values may be sent and summed in bfloat16 or wider, within the bound.
No kernel may reach another device: no remote copies, remote signals or barrier semaphores. Data moves between devices by JAX's collectives and lax.ppermute only.
A program may use at most 128 MiB of HBM per device.

v0:
```python
import jax
import jax.numpy as jnp
from jax import lax
from jax.sharding import PartitionSpec as P

CAP = 5


adam_rate = 0.01
beta_one = 0.9
beta_two = 0.999
adam_step = 100.0
adam_eps = 1e-08


def swapped_2(array, axis, stride):
    return lax.ppermute(array, axis, [(i, i ^ 1 << stride) for i in range(lax.axis_size(axis))])


def contract(left_side, right_side, left_dim, right_dim):
    return lax.dot_general(
        left_side,
        right_side,
        (((left_dim,), (right_dim,)), ((), ())),
        preferred_element_type=jnp.float32,
    )


def forward_rows(token_rows, w_gate, w_up):
    gate_proj = contract(token_rows, w_gate, 1, 1)
    up_proj = contract(token_rows, w_up, 1, 1)
    sigmoid_val = jax.nn.sigmoid(gate_proj)
    activated = gate_proj * sigmoid_val
    slopes = sigmoid_val * (1.0 + gate_proj * (1.0 - sigmoid_val))
    hidden = (activated * up_proj).astype(jnp.bfloat16)
    return (up_proj, activated, slopes, hidden)


def backward_rows(token_rows, grad_rows, up_proj, activated, slopes, hidden, w_dn):
    back_grad = contract(grad_rows, w_dn, 1, 1)
    gate_back = (back_grad * up_proj * slopes).astype(jnp.bfloat16)
    up_back = (back_grad * activated).astype(jnp.bfloat16)
    return (
        contract(hidden, grad_rows, 0, 0),
        contract(gate_back, token_rows, 0, 0),
        contract(up_back, token_rows, 0, 0),
    )


def add_terms(new_terms):
    return tuple((term_part for term_part in new_terms))


def section_take(swap_code, slot_value, section_bit):
    partner_slot = jnp.bitwise_xor(slot_value, 1 << section_bit)
    lower_slot = jnp.minimum(slot_value, partner_slot)
    return jnp.take(swap_code, lower_slot) // (1 << section_bit) % 2 == 1


def local(tokens, grad_out, route_weights, expert_ids, swap_code, w_in, w_down, moment1, moment2):
    expert_count = lax.axis_size("expert")
    section_count = expert_count.bit_length() - 1
    own_slot = lax.axis_index("expert")
    slot_ids = jnp.arange(expert_count, dtype=jnp.int32)
    expert_state = (w_in, w_down, moment1, moment2)
    weight_in, weight_down, moment_one, moment_two = expert_state
    local_rows, top_count = expert_ids.shape
    flat_ids = expert_ids.reshape(-1)
    inside = flat_ids < expert_count
    target_slot = jnp.sum(
        jnp.where(flat_ids[:, None] == slot_ids[None, :], slot_ids[None, :], 0), axis=1
    )
    in_bucket = jnp.logical_and(target_slot[:, None] == slot_ids[None, :], inside[:, None]).astype(
        jnp.int32
    )
    bucket_rank = jnp.sum((jnp.cumsum(in_bucket, axis=0) - 1) * in_bucket, axis=1)
    slot_number = jnp.where(inside, target_slot * CAP + bucket_rank, -1)
    bucket_ids = jnp.arange(expert_count * CAP, dtype=jnp.int32)
    matched = slot_number[None, :] == bucket_ids[:, None]
    copy_row = jnp.arange(local_rows * top_count, dtype=jnp.int32) // top_count
    source_row = jnp.sum(jnp.where(matched, copy_row[None, :], 0), axis=1)
    filled = jnp.any(matched, axis=1)
    row_scale = jnp.sum(jnp.where(matched, route_weights.reshape(-1)[None, :], 0.0), axis=1)
    tok_send = jnp.where(
        filled[:, None], jnp.take(tokens, source_row, axis=0), jnp.zeros((), jnp.bfloat16)
    )
    grad_send = (
        jnp.take(grad_out, source_row, axis=0).astype(jnp.float32) * row_scale[:, None]
    ).astype(jnp.bfloat16)
    tok_recv, grad_recv = (
        lax.all_to_all(tok_send, "expert", split_axis=0, concat_axis=0, tiled=True),
        lax.all_to_all(grad_send, "expert", split_axis=0, concat_axis=0, tiled=True),
    )
    w_gate = weight_in[0, 0]
    w_up = weight_in[0, 1]
    w_dn = weight_down[0]
    token_rows = lax.all_gather(tok_recv, "dp", axis=0, tiled=True)
    grad_rows = lax.all_gather(grad_recv, "dp", axis=0, tiled=True)
    up_proj, activated, slopes, hidden = forward_rows(token_rows, w_gate, w_up)
    down_grad, gate_grad, up_grad = add_terms(
        backward_rows(token_rows, grad_rows, up_proj, activated, slopes, hidden, w_dn)
    )
    first_new = beta_one * moment_one + (1.0 - beta_one) * down_grad[None]
    second_new = beta_two * moment_two + (1.0 - beta_two) * (down_grad * down_grad)[None]
    fix_one = 1.0 - beta_one**adam_step
    fix_two = 1.0 - beta_two**adam_step
    step_size = first_new / fix_one / (jnp.sqrt(second_new / fix_two) + adam_eps)
    down_new = (weight_down.astype(jnp.float32) - adam_rate * step_size).astype(jnp.bfloat16)
    grad_new = jnp.stack([gate_grad, up_grad])[None].astype(jnp.bfloat16)
    outputs = (down_new, first_new, second_new, grad_new)
    for section_bit in range(section_count):
        partner_out = swapped_2(outputs, "expert", section_bit)
        swapped = section_take(swap_code, own_slot, section_bit)
        outputs = tuple(
            (jnp.where(swapped, theirs, own_part) for theirs, own_part in zip(partner_out, outputs))
        )
    return outputs


def solution(mesh):
    placed = (
        P(("expert", "dp"), None),
        P(("expert", "dp"), None),
        P(("expert", "dp"), None),
        P(("expert", "dp"), None),
        P(),
        P("expert", None, "dp", None),
        P("expert", "dp", None),
        P("expert", "dp", None),
        P("expert", "dp", None),
    )
    return jax.shard_map(
        local,
        mesh=mesh,
        in_specs=placed,
        out_specs=(
            P("expert", "dp", None),
            P("expert", "dp", None),
            P("expert", "dp", None),
            P("expert", None, "dp", None),
        ),
        check_vma=False,
    )
```

profile of v0, /device:TPU:0, one launch (start us, length us, event | category | flops | bytes accessed | tf_op | source)
XLA Modules:
  0.0 422.2 jit_solution(6011747193033548992)
XLA Ops:
  12.0 9.7 %all_to_all.24 = bf16[4,5,3584]{2,1,0:T(8,128)(2,1)S(1)} all-to-all(bf16[4,5,3584]{2,1,0:T(8,128)(2,1)S(1)} %all_to_all.16), channel_id=1, replica_groups=mesh['expert'=4,'dp'=8] {'expert'}, dimensions={0} | all-to-all | bytes 286720 | tf_op jit(solution)/shard_map/all_to_all | solution.py:91
  23.7 8.1 %all_to_all.25 = bf16[4,5,3584]{2,1,0:T(8,128)(2,1)S(1)} all-to-all(bf16[4,5,3584]{2,1,0:T(8,128)(2,1)S(1)} %all_to_all.19), channel_id=1, replica_groups=mesh['expert'=4,'dp'=8] {'expert'}, dimensions={0} | all-to-all | bytes 286720 | tf_op jit(solution)/shard_map/all_to_all | solution.py:92
  32.5 32.7 %all-gather.5.cloned.1.call-done = bf16[8,20,3584]{2,1,0:T(8,128)(2,1)} async-done(((bf16[1,20,3584]{2,1,0:T(8,128)(2,1)}), bf16[8,20,3584]{2,1,0:T(8,128)(2,1)}) %all-gather.5.cloned.1.call-update) | async-done | bytes 1146896 | tf_op jit(solution)/shard_map/all_gather | solution.py:97
  66.7 2.2 fusion.6
  68.9 2.2 fusion.4
  71.2 37.7 %all-gather.7.cloned.1.call-done = bf16[8,20,3584]{2,1,0:T(8,128)(2,1)} async-done(((bf16[1,20,3584]{2,1,0:T(8,128)(2,1)}), bf16[8,20,3584]{2,1,0:T(8,128)(2,1)}) %all-gather.7.cloned.1.call-update) | async-done | bytes 1146896 | tf_op jit(solution)/shard_map/all_gather | solution.py:98
  111.3 2.2 fusion.2
  115.0 2.2 pad_maximum_fusion
  120.3 5.3 %subtract_convert_fusion = (bf16[1,256,3584]{2,1,0:T(8,128)(2,1)}, f32[1,256,3584]{2,1,0:T(8,128)}, f32[1,256,3584]{2,1,0:T(8,128)}) fusion(bf16[1,256,3584]{2,1,0:T(8,128)(2,1)S(1)} %copy-done.8, f32[1,256,3584]{2,1,0:T(8,128)S(1)} %copy-done.11, f32[1,256,3584]{2,1,0:T(8,128)S(1)} %copy-done.12, bf16[160,3584]{1,0:T(8,128)(2,1)S(1)} %copy-done.6, ...), kind=kOutput, calls=%fused_computation.9 | convolution fusion | flops 307609600 | bytes 19824640 | tf_op jit(solution)/shard_map/dot_general | solution.py:21
  127.5 2.2 collective-permute-done
  129.8 2.9 broadcast_select_fusion.4
  132.7 1.5 collective-permute-start.1
  134.2 4.3 %broadcast_select_fusion = bf16[1,2,256,3584]{3,2,1,0:T(8,128)(2,1)} fusion(bf16[1,2,256,3584]{3,2,1,0:T(8,128)(2,1)} %collective-permute-done.6, pred[]{:T(512)S(6)} %eq.61, bf16[1,1,256,3584]{3,2,1,0:T(8,128)(2,1)S(1)} %fusion.1, bf16[1,1,256,3584]{3,2,1,0:T(8,128)(2,1)S(1)} %copy-done.3), kind=kLoop, calls=%fused_computation.10 | loop fusion | flops 3670016 | bytes 11010049 | tf_op jit(solution)/shard_map/jit(_where)/select_n | solution.py:115
  139.0 4.3 %broadcast_select_fusion.3 = f32[1,256,3584]{2,1,0:T(8,128)} fusion(f32[1,256,3584]{2,1,0:T(8,128)} %collective-permute-done.2, f32[1,256,3584]{2,1,0:T(8,128)} %get-tuple-element.28, pred[]{:T(512)S(6)} %eq.61), kind=kLoop, calls=%fused_computation.21 | loop fusion | flops 917504 | bytes 11010049 | tf_op jit(solution)/shard_map/jit(_where)/select_n | solution.py:115
  143.3 1.5 collective-permute-start.3
  144.8 4.3 %broadcast_select_fusion.2 = f32[1,256,3584]{2,1,0:T(8,128)} fusion(f32[1,256,3584]{2,1,0:T(8,128)} %collective-permute-done.4, f32[1,256,3584]{2,1,0:T(8,128)} %get-tuple-element.29, pred[]{:T(512)S(6)} %eq.61), kind=kLoop, calls=%fused_computation.20 | loop fusion | flops 917504 | bytes 11010049 | tf_op jit(solution)/shard_map/jit(_where)/select_n | solution.py:115
  150.3 25.5 %collective-permute-done.1 = bf16[1,256,3584]{2,1,0:T(8,128)(2,1)} collective-permute-done((bf16[1,256,3584]{2,1,0:T(8,128)(2,1)}, bf16[1,256,3584]{2,1,0:T(8,128)(2,1)}, u32[]{:S(2)}, u32[]{:S(2)}) %collective-permute-start.1) | collective-permute-done | bytes 1835040 | tf_op jit(solution)/shard_map/ppermute | solution.py:17
  175.9 2.9 broadcast_select_fusion.7
  178.8 75.7 %collective-permute-done.7 = bf16[1,2,256,3584]{3,2,1,0:T(8,128)(2,1)} collective-permute-done((bf16[1,2,256,3584]{3,2,1,0:T(8,128)(2,1)}, bf16[1,2,256,3584]{3,2,1,0:T(8,128)(2,1)}, u32[]{:S(2)}, u32[]{:S(2)}) %collective-permute-start.7) | collective-permute-done | bytes 3670048 | tf_op jit(solution)/shard_map/ppermute | solution.py:17
  254.5 4.6 %broadcast_select_fusion.1 = bf16[1,2,256,3584]{3,2,1,0:T(8,128)(2,1)} fusion(bf16[1,2,256,3584]{3,2,1,0:T(8,128)(2,1)} %collective-permute-done.7, pred[]{:T(512)S(6)} %eq.60, bf16[1,2,256,3584]{3,2,1,0:T(8,128)(2,1)} %collective-permute-done.6, bf16[1,1,256,3584]{3,2,1,0:T(8,128)(2,1)S(1)} %fusion.1, bf16[1,1,256,3584]{3,2,1,0:T(8,128)(2,1)S(1)} %copy-done.4, ...), kind=kLoop, calls=%fused_computation.11 | loop fusion | flops 5505024 | bytes 14680066 | tf_op jit(solution)/shard_map/jit(_where)/select_n | solution.py:115
  259.1 74.0 %collective-permute-done.3 = f32[1,256,3584]{2,1,0:T(8,128)} collective-permute-done((f32[1,256,3584]{2,1,0:T(8,128)}, f32[1,256,3584]{2,1,0:T(8,128)}, u32[]{:S(2)}, u32[]{:S(2)}) %collective-permute-start.3) | collective-permute-done | bytes 3670048 | tf_op jit(solution)/shard_map/ppermute | solution.py:17
  333.2 4.4 %broadcast_select_fusion.6 = f32[1,256,3584]{2,1,0:T(8,128)} fusion(f32[1,256,3584]{2,1,0:T(8,128)} %collective-permute-done.3, f32[1,256,3584]{2,1,0:T(8,128)} %broadcast_select_fusion.3, pred[]{:T(512)S(6)} %eq.60), kind=kLoop, calls=%fused_computation.24 | loop fusion | flops 917504 | bytes 11010049 | tf_op jit(solution)/shard_map/jit(_where)/select_n | solution.py:115
  337.5 73.5 %collective-permute-done.5 = f32[1,256,3584]{2,1,0:T(8,128)} collective-permute-done((f32[1,256,3584]{2,1,0:T(8,128)}, f32[1,256,3584]{2,1,0:T(8,128)}, u32[]{:S(2)}, u32[]{:S(2)}) %collective-permute-start.5) | collective-permute-done | bytes 3670048 | tf_op jit(solution)/shard_map/ppermute | solution.py:17
  411.0 4.3 %broadcast_select_fusion.5 = f32[1,256,3584]{2,1,0:T(8,128)} fusion(f32[1,256,3584]{2,1,0:T(8,128)} %collective-permute-done.5, f32[1,256,3584]{2,1,0:T(8,128)} %broadcast_select_fusion.2, pred[]{:T(512)S(6)} %eq.60), kind=kLoop, calls=%fused_computation.23 | loop fusion | flops 917504 | bytes 11010049 | tf_op jit(solution)/shard_map/jit(_where)/select_n | solution.py:115
  (74 shorter events, 18.1 us)
Async XLA Ops:
  7.2 4.0 copy-start
  7.2 15.3 %copy-start.9 = (f32[128,8]{0,1:T(8,128)S(1)}, f32[128,8]{0,1:T(8,128)}, u32[]{:S(2)}) copy-start(f32[128,8]{0,1:T(8,128)} %param.13) | copy-start | bytes 12292
  7.2 15.5 %copy-start.7 = (bf16[128,3584]{1,0:T(8,128)(2,1)S(1)}, bf16[128,3584]{1,0:T(8,128)(2,1)}, u32[]{:S(2)}) copy-start(bf16[128,3584]{1,0:T(8,128)(2,1)} %param.12) | copy-start | bytes 2752516
  7.2 58.0 %all-gather.5.cloned.1.call-start = ((), (), s32[]{:S(2)}) async-start(), calls=%async_computation.2 | async-start | bytes 1548288 | tf_op jit(solution)/shard_map/all_gather | solution.py:97
  22.5 86.4 %all-gather.7.cloned.1.call-start = ((), (), s32[]{:S(2)}) async-start(), calls=%async_computation.3 | async-start | bytes 1548288 | tf_op jit(solution)/shard_map/all_gather | solution.py:98
  110.3 1.0 copy-start.5
  114.3 3.5 copy-start.12
  115.0 2.8 copy-start.2
  115.0 3.5 copy-start.6
  115.0 4.2 %copy-start.8 = (bf16[1,256,3584]{2,1,0:T(8,128)(2,1)S(1)}, bf16[1,256,3584]{2,1,0:T(8,128)(2,1)}, u32[]{:S(2)}) copy-start(bf16[1,256,3584]{2,1,0:T(8,128)(2,1)} %param.17) | copy-start | bytes 5505028
  115.0 5.3 %copy-start.11 = (f32[1,256,3584]{2,1,0:T(8,128)S(1)}, f32[1,256,3584]{2,1,0:T(8,128)}, u32[]{:S(2)}) copy-start(f32[1,256,3584]{2,1,0:T(8,128)} %param.18) | copy-start | bytes 11010052
  117.8 8.4 %copy-start.10 = (s32[4]{0:T(128)S(1)}, s32[4]{0:T(128)}, u32[]{:S(2)}) copy-start(s32[4]{0:T(128)} %param.15) | copy-start | bytes 52
  117.8 16.4 %collective-permute-start.6 = (bf16[1,2,256,3584]{3,2,1,0:T(8,128)(2,1)}, bf16[1,2,256,3584]{3,2,1,0:T(8,128)(2,1)}, u32[]{:S(2)}, u32[]{:S(2)}) collective-permute-start(bf16[1,2,256,3584]{3,2,1,0:T(8,128)(2,1)} %pad_maximum_fusion), channel_id=1, source_target_pairs={{0,8},{8,0},{16,24},{24,16},{1,9},{9,1},{17,25},{25,17},{2,10},{10... | collective-permute-start | bytes 11010056 | tf_op jit(solution)/shard_map/ppermute | solution.py:17
  125.6 4.1 collective-permute-start
  125.6 13.4 %collective-permute-start.2 = (f32[1,256,3584]{2,1,0:T(8,128)}, f32[1,256,3584]{2,1,0:T(8,128)}, u32[]{:S(2)}, u32[]{:S(2)}) collective-permute-start(f32[1,256,3584]{2,1,0:T(8,128)} %get-tuple-element.28), channel_id=1, source_target_pairs={{0,8},{8,0},{16,24},{24,16},{1,9},{9,1},{17,25},{25,17},{2,10},{10... | collective-permute-start | bytes 11010056 | tf_op jit(solution)/shard_map/ppermute | solution.py:17
  126.1 18.7 %collective-permute-start.4 = (f32[1,256,3584]{2,1,0:T(8,128)}, f32[1,256,3584]{2,1,0:T(8,128)}, u32[]{:S(2)}, u32[]{:S(2)}) collective-permute-start(f32[1,256,3584]{2,1,0:T(8,128)} %get-tuple-element.29), channel_id=1, source_target_pairs={{0,8},{8,0},{16,24},{24,16},{1,9},{9,1},{17,25},{25,17},{2,10},{10... | collective-permute-start | bytes 11010056 | tf_op jit(solution)/shard_map/ppermute | solution.py:17
  127.5 6.6 %copy-start.3 = (bf16[1,1,256,3584]{3,2,1,0:T(8,128)(2,1)S(1)}, bf16[1,1,256,3584]{3,2,1,0:T(8,128)(2,1)}, u32[]{:S(2)}) copy-start(bf16[1,1,256,3584]{3,2,1,0:T(8,128)(2,1)} %copy-done.2) | copy-start | bytes 5505028
  132.7 43.2 %collective-permute-start.1 = (bf16[1,256,3584]{2,1,0:T(8,128)(2,1)}, bf16[1,256,3584]{2,1,0:T(8,128)(2,1)}, u32[]{:S(2)}, u32[]{:S(2)}) collective-permute-start(bf16[1,256,3584]{2,1,0:T(8,128)(2,1)} %broadcast_select_fusion.4), channel_id=1, source_target_pairs={{0,16},{8,24},{16,0},{24,8},{1,17},{9,25},{17,1},{25,9},{2,18},{10... | collective-permute-start | bytes 5505032 | tf_op jit(solution)/shard_map/ppermute | solution.py:17
  138.5 116.0 %collective-permute-start.7 = (bf16[1,2,256,3584]{3,2,1,0:T(8,128)(2,1)}, bf16[1,2,256,3584]{3,2,1,0:T(8,128)(2,1)}, u32[]{:S(2)}, u32[]{:S(2)}) collective-permute-start(bf16[1,2,256,3584]{3,2,1,0:T(8,128)(2,1)} %broadcast_select_fusion), channel_id=1, source_target_pairs={{0,16},{8,24},{16,0},{24,8},{1,17},{9,25},{17,1},{25,9},{2,18},{10... | collective-permute-start | bytes 11010056 | tf_op jit(solution)/shard_map/ppermute | solution.py:17
  143.3 189.8 %collective-permute-start.3 = (f32[1,256,3584]{2,1,0:T(8,128)}, f32[1,256,3584]{2,1,0:T(8,128)}, u32[]{:S(2)}, u32[]{:S(2)}) collective-permute-start(f32[1,256,3584]{2,1,0:T(8,128)} %broadcast_select_fusion.3), channel_id=1, source_target_pairs={{0,16},{8,24},{16,0},{24,8},{1,17},{9,25},{17,1},{25,9},{2,18},{10... | collective-permute-start | bytes 11010056 | tf_op jit(solution)/shard_map/ppermute | solution.py:17
  149.1 261.9 %collective-permute-start.5 = (f32[1,256,3584]{2,1,0:T(8,128)}, f32[1,256,3584]{2,1,0:T(8,128)}, u32[]{:S(2)}, u32[]{:S(2)}) collective-permute-start(f32[1,256,3584]{2,1,0:T(8,128)} %broadcast_select_fusion.2), channel_id=1, source_target_pairs={{0,16},{8,24},{16,0},{24,8},{1,17},{9,25},{17,1},{25,9},{2,18},{10... | collective-permute-start | bytes 11010056 | tf_op jit(solution)/shard_map/ppermute | solution.py:17
  150.3 104.2 %copy-start.4 = (bf16[1,1,256,3584]{3,2,1,0:T(8,128)(2,1)S(1)}, bf16[1,1,256,3584]{3,2,1,0:T(8,128)(2,1)}, u32[]{:S(2)}) copy-start(bf16[1,1,256,3584]{3,2,1,0:T(8,128)(2,1)} %copy-done.2) | copy-start | bytes 5505028
  333.2 82.2 %copy-start.1 = (bf16[128,3584]{1,0:T(8,128)(2,1)S(1)}, bf16[128,3584]{1,0:T(8,128)(2,1)}, u32[]{:S(2)}) copy-start(bf16[128,3584]{1,0:T(8,128)(2,1)} %param.11) | copy-start | bytes 2752516
Sparse Core Ops, SparseCore 0:
  22.6 42.5 all-gather.4
  68.0 40.8 all-gather.6
where the time goes:
time: 423 us; the launch traced here: 422 us
  waiting for transfers between devices  321 us (76%)
  other arithmetic  37.2 us (9%)
  blocking collectives  17.8 us (4%)
  between operations  15.6 us (4%)
  matrix products  13.4 us (3%)
  local copies, waits for them, and re-layouts  12.1 us (3%)
  starting transfers between devices  4.65 us (1%)
    ppermute x8, waiting for transfers between devices, swapped_2(): lax.ppermute(array, axis, [(i, i ^ 1 << stride) for i in range(lax.axis_s...  251 us
    all_gather x1, waiting for transfers between devices, local(): grad_rows = lax.all_gather(grad_recv, 'dp', axis=0, tiled=True)  37.7 us
    all_gather x1, waiting for transfers between devices, local(): token_rows = lax.all_gather(tok_recv, 'dp', axis=0, tiled=True)  32.7 us
    select_n x8, other arithmetic, local(): jnp.where(swapped, theirs, own_part)  32.1 us
    dot_general x6, matrix products, contract(): lax.dot_general(left_side, right_side, (((left_dim,), (right_dim,)), ((),...  13.4 us
    all_to_all x1, blocking collectives, local(): lax.all_to_all(tok_send, 'expert', split_axis=0, concat_axis=0, tiled=True)  9.72 us
    unnamed x32, local copies, waits for them, and re-layouts  9.36 us
  transfers between devices with their start and end apart: 10, of which 7 were waited for; matrix products, arithmetic and copies ran while one was open for 10% of the time, Pallas kernels for 0%

commit v1 on v0

v1 whole, which is shorter than its diff:
```python
import functools
import itertools

import jax
import jax.numpy as jnp
from jax import lax
from jax.experimental import pallas as pl
from jax.experimental.pallas import tpu as pltpu
from jax.sharding import PartitionSpec as P

CAP = 5
VMEM_LIMIT = 40 * 1024 * 1024

adam_rate = 0.01
beta_one = 0.9
beta_two = 0.999
adam_step = 100.0
adam_eps = 1e-08


def dot(left_side, right_side, left_dim, right_dim):
    return lax.dot_general(
        left_side,
        right_side,
        (((left_dim,), (right_dim,)), ((), ())),
        preferred_element_type=jnp.float32,
    )


def params():
    return pltpu.CompilerParams(vmem_limit_bytes=VMEM_LIMIT)


def cost(flops, nbytes):
    return pl.CostEstimate(flops=int(flops), bytes_accessed=int(nbytes), transcendentals=0)


def tile_of(width, most):
    tile = 128
    for count in range(1, width // 128 + 1):
        if width % (count * 128) == 0 and count * 128 <= most:
            tile = count * 128
    return tile


def pick_kernel(expert_count, ids_ref, weights_ref, tok_ref, grad_ref, out_ref, sel_t, sel_g, scale):
    rows = tok_ref.shape[0]
    half = expert_count * CAP

    @pl.when(pl.program_id(0) == 0)
    def _():
        ids = ids_ref[...]
        weights = weights_ref[...]
        earlier = (
            lax.broadcasted_iota(jnp.int32, (rows, rows), 0)
            < lax.broadcasted_iota(jnp.int32, (rows, rows), 1)
        ).astype(jnp.bfloat16)
        row = lax.broadcasted_iota(jnp.int32, (2 * half, rows), 0)
        in_half = jnp.where(row >= half, row - half, row)
        chosen = jnp.zeros((2 * half, rows), jnp.float32)
        weight = jnp.zeros((2 * half, rows), jnp.float32)
        for expert in range(expert_count):
            named = ids == expert
            hit = jnp.max(jnp.where(named, 1.0, 0.0), axis=0, keepdims=True)
            amount = jnp.sum(jnp.where(named, weights, 0.0), axis=0, keepdims=True)
            hits = jnp.broadcast_to(hit, (8, rows))
            rank = dot(hits.astype(jnp.bfloat16), earlier, 1, 0)[0:1].astype(jnp.int32)
            of_expert = jnp.logical_and(in_half >= expert * CAP, in_half < (expert + 1) * CAP)
            match = jnp.logical_and(of_expert, in_half - expert * CAP == rank)
            chosen = chosen + jnp.where(match, hit, 0.0)
            weight = weight + jnp.where(match, hit * amount, 0.0)
        is_token = row < half
        sel_t[...] = jnp.where(is_token, chosen, 0.0).astype(jnp.bfloat16)
        sel_g[...] = jnp.where(is_token, 0.0, chosen).astype(jnp.bfloat16)
        scale[...] = jnp.sum(weight, axis=1, keepdims=True)

    picked = dot(sel_t[...], tok_ref[...], 1, 0) + scale[...] * dot(sel_g[...], grad_ref[...], 1, 0)
    out_ref[...] = picked.astype(jnp.bfloat16)


def pick_rows(tokens, grad_out, route_weights, expert_ids, expert_count):
    rows, width = tokens.shape
    top = expert_ids.shape[1]
    total = 2 * expert_count * CAP
    tile = tile_of(width, 1792)
    return pl.pallas_call(
        functools.partial(pick_kernel, expert_count),
        grid=(width // tile,),
        in_specs=[
            pl.BlockSpec((top, rows), lambda j: (0, 0)),
            pl.BlockSpec((top, rows), lambda j: (0, 0)),
            pl.BlockSpec((rows, tile), lambda j: (0, j)),
            pl.BlockSpec((rows, tile), lambda j: (0, j)),
        ],
        out_specs=pl.BlockSpec((total, tile), lambda j: (0, j)),
        out_shape=jax.ShapeDtypeStruct((total, width), jnp.bfloat16),
        scratch_shapes=[
            pltpu.VMEM((total, rows), jnp.bfloat16),
            pltpu.VMEM((total, rows), jnp.bfloat16),
            pltpu.VMEM((total, 1), jnp.float32),
        ],
        compiler_params=params(),
        cost_estimate=cost(4 * total * rows * width, 4 * rows * width),
        name="pick_rows",
    )(expert_ids.T, route_weights.T, tokens, grad_out)


def factor_kernel(half, x_ref, w_in_ref, w_down_ref, out_ref, acc):
    step = pl.program_id(0)
    count, units = acc.shape[0], w_down_ref.shape[1]

    @pl.when(step == 0)
    def _():
        acc[...] = jnp.zeros_like(acc)

    x = x_ref[...]
    acc[:, 0:units] += dot(x, w_in_ref[0, 0], 1, 1)
    acc[:, units : 2 * units] += dot(x, w_in_ref[0, 1], 1, 1)
    acc[:, 2 * units : 3 * units] += dot(x, w_down_ref[0], 1, 1)

    @pl.when(step == pl.num_programs(0) - 1)
    def _():
        gate = acc[:, 0:units]
        up = acc[:, units : 2 * units]
        back = pltpu.roll(acc[:, 2 * units : 3 * units], count - half, 0)
        sig = jax.nn.sigmoid(gate)
        activated = gate * sig
        slopes = sig * (1.0 + gate * (1.0 - sig))
        hidden = pltpu.roll(activated * up, half, 0)
        is_token = lax.broadcasted_iota(jnp.int32, (count, units), 0) % (2 * half) < half
        out_ref[:, 0:units] = jnp.where(is_token, back * up * slopes, hidden).astype(jnp.bfloat16)
        out_ref[:, units : 2 * units] = jnp.where(is_token, back * activated, 0.0).astype(jnp.bfloat16)


def factors_of(x, w_in, w_down, half):
    count, width = x.shape
    units = w_down.shape[1]
    tile = tile_of(width, 896)
    return pl.pallas_call(
        functools.partial(factor_kernel, half),
        grid=(width // tile,),
        in_specs=[
            pl.BlockSpec((count, tile), lambda j: (0, j)),
            pl.BlockSpec((1, 2, units, tile), lambda j: (0, 0, 0, j)),
            pl.BlockSpec((1, units, tile), lambda j: (0, 0, j)),
        ],
        out_specs=pl.BlockSpec((count, 2 * units), lambda j: (0, 0)),
        out_shape=jax.ShapeDtypeStruct((count, 2 * units), jnp.bfloat16),
        scratch_shapes=[pltpu.VMEM((count, 3 * units), jnp.float32)],
        compiler_params=params(),
        cost_estimate=cost(6 * count * units * width, 6 * units * width + 2 * count * width),
        name="factors",
    )(x, w_in, w_down)


def grad_kernel(half, factor_ref, x_ref, out_ref):
    count, units = factor_ref.shape[0], out_ref.shape[2]
    is_token = lax.broadcasted_iota(jnp.int32, (count, units), 0) % (2 * half) < half
    both = factor_ref[:, 0:units]
    gate_back = jnp.where(is_token, both, jnp.zeros_like(both))
    x = x_ref[...]
    out_ref[0, 0] = dot(gate_back, x, 0, 0).astype(jnp.bfloat16)
    out_ref[0, 1] = dot(factor_ref[:, units : 2 * units], x, 0, 0).astype(jnp.bfloat16)


def grads_of(factors, x, half):
    count, width = x.shape
    units = factors.shape[1] // 2
    tile = tile_of(width, 896)
    return pl.pallas_call(
        functools.partial(grad_kernel, half),
        grid=(width // tile,),
        in_specs=[
            pl.BlockSpec((count, 2 * units), lambda j: (0, 0)),
            pl.BlockSpec((count, tile), lambda j: (0, j)),
        ],
        out_specs=pl.BlockSpec((1, 2, units, tile), lambda j: (0, 0, 0, j)),
        out_shape=jax.ShapeDtypeStruct((1, 2, units, width), jnp.bfloat16),
        compiler_params=params(),
        cost_estimate=cost(4 * count * units * width, 4 * units * width + 2 * count * width),
        name="in_grads",
    )(factors, x)


def pack_kernel(w_ref, one_ref, two_ref, out_ref):
    out_ref[0] = w_ref[0]
    out_ref[1] = one_ref[0].astype(jnp.bfloat16)
    out_ref[2] = two_ref[0].astype(jnp.bfloat16)


def pack(w_down, moment1, moment2, chunk, chunks):
    _, units, width = w_down.shape
    rows = units // chunks
    tile = tile_of(width, 1792)
    spec = pl.BlockSpec((1, rows, tile), lambda j: (0, chunk, j))
    return pl.pallas_call(
        pack_kernel,
        grid=(width // tile,),
        in_specs=[spec, spec, spec],
        out_specs=pl.BlockSpec((3, rows, tile), lambda j: (0, 0, j)),
        out_shape=jax.ShapeDtypeStruct((3, rows, width), jnp.bfloat16),
        compiler_params=params(),
        cost_estimate=cost(2 * rows * width, 16 * rows * width),
        name=f"pack_state_{chunk}",
    )(w_down, moment1, moment2)


def adam_kernel(half, chunk, factor_ref, x_ref, state_ref, *refs):
    down_ref, one_ref, two_ref = refs[-3:]
    count, rows = x_ref.shape[0], state_ref.shape[1]
    is_token = lax.broadcasted_iota(jnp.int32, (count, rows), 0) % (2 * half) < half
    both = factor_ref[:, chunk * rows : (chunk + 1) * rows]
    hidden = jnp.where(is_token, jnp.zeros_like(both), both)
    down_grad = dot(hidden, x_ref[...], 0, 0)
    first_new = beta_one * state_ref[1].astype(jnp.float32) + (1.0 - beta_one) * down_grad
    second_new = beta_two * state_ref[2].astype(jnp.float32) + (1.0 - beta_two) * (down_grad * down_grad)
    fix_one = 1.0 - beta_one**adam_step
    fix_two = 1.0 - beta_two**adam_step
    step_size = first_new / fix_one / (jnp.sqrt(second_new / fix_two) + adam_eps)
    down_ref[0] = (state_ref[0].astype(jnp.float32) - adam_rate * step_size).astype(jnp.bfloat16)
    one_ref[0] = first_new
    two_ref[0] = second_new


def adam_rows(factors, x, state, chunk, chunks, half, before):
    count, width = x.shape
    units = factors.shape[1] // 2
    rows = units // chunks
    tile = tile_of(width, 896)
    spec = pl.BlockSpec((1, rows, tile), lambda j: (0, chunk, j))
    shapes = tuple(
        jax.ShapeDtypeStruct((1, units, width), kind) for kind in (jnp.bfloat16, jnp.float32, jnp.float32)
    )
    return pl.pallas_call(
        functools.partial(adam_kernel, half, chunk),
        grid=(width // tile,),
        in_specs=[
            pl.BlockSpec((count, 2 * units), lambda j: (0, 0)),
            pl.BlockSpec((count, tile), lambda j: (0, j)),
            pl.BlockSpec((3, rows, tile), lambda j: (0, 0, j)),
        ]
        + [pl.BlockSpec(memory_space=pl.ANY)] * len(before),
        out_specs=[spec, spec, spec],
        out_shape=shapes,
        input_output_aliases={3 + i: i for i in range(len(before))},
        compiler_params=params(),
        cost_estimate=cost(2 * count * rows * width, 16 * rows * width + 2 * count * width),
        name=f"adam_rows_{chunk}",
    )(factors, x, state, *before)


def shifted(array, axis_sizes, which, amount):
    planes, columns = axis_sizes
    pairs = []
    for plane, column in itertools.product(range(planes), range(columns)):
        if which == 0:
            target = (plane + amount) % planes * columns + column
        else:
            target = plane * columns + (column + amount) % columns
        pairs.append((plane * columns + column, target))
    return lax.ppermute(array, "dp", pairs)


def gather_dp(block, axis_sizes):
    planes, columns = axis_sizes
    parts = [block] + [shifted(block, axis_sizes, 0, k) for k in range(1, planes)]
    parts = parts + [shifted(p, axis_sizes, 1, k) for k in range(1, columns) for p in parts]
    return jnp.concatenate(parts, axis=0)


def role_block(pieces, masks, experts, own_slot, expert_count):
    half = expert_count * CAP
    total = 2 * half
    row = jnp.arange(total, dtype=jnp.int32)
    is_grad = row // half
    contributor = row % half // CAP
    place = jnp.zeros_like(row)
    for number, mask in enumerate(masks):
        place = jnp.where(contributor == jnp.bitwise_xor(own_slot, mask), number, place)
    column = jnp.arange(len(masks) * total, dtype=jnp.int32)
    blocks = []
    for expert in experts:
        wanted = place * total + is_grad * half + expert * CAP + row % CAP
        chosen = (wanted[:, None] == column[None, :]).astype(jnp.bfloat16)
        blocks.append(dot(chosen, pieces, 1, 0).astype(jnp.bfloat16))
    return blocks


def section_swaps(swap_code, slot, sections):
    swaps = []
    for bit in range(sections):
        lower = jnp.minimum(slot, jnp.bitwise_xor(slot, 1 << bit))
        swaps.append(swap_code[lower] // (1 << bit) % 2 == 1)
    return swaps


def static_order(expert_count, sections, swapped_pairs):
    order = list(range(expert_count))
    for bit in range(sections):
        step = [s ^ (1 << bit) if (bit, min(s, s ^ (1 << bit))) in swapped_pairs else s for s in range(expert_count)]
        order = [order[s] for s in step]
    return order


def exchange(picked, sections):
    pieces, masks = [picked], [0]
    for bit in reversed(range(sections)):
        pairs = [(i, i ^ (1 << bit)) for i in range(1 << sections)]
        theirs = lax.ppermute(jnp.concatenate(pieces, axis=0), "expert", pairs)
        size = picked.shape[0]
        pieces = pieces + [theirs[i * size : (i + 1) * size] for i in range(len(pieces))]
        masks = masks + [m ^ (1 << bit) for m in masks]
    return jnp.concatenate(pieces, axis=0), masks


def layer(move, axis_sizes, sections, chunks, picked, source, w_in, w_down, moment1, moment2):
    expert_count = 1 << sections
    half = expert_count * CAP
    own_slot = lax.axis_index("expert")
    states = [move(pack(w_down, moment1, moment2, c, chunks)) for c in range(chunks)]
    pieces, masks = exchange(picked, sections)
    own_block, new_block = role_block(pieces, masks, (own_slot, source), own_slot, expert_count)
    own_rows = gather_dp(own_block, axis_sizes)
    factors = factors_of(own_rows, w_in, w_down, half)
    new_rows = gather_dp(new_block, axis_sizes)
    factors = move(factors)
    grads = grads_of(factors, new_rows, half)
    outputs = ()
    for c in range(chunks):
        outputs = adam_rows(factors, new_rows, states[c], c, chunks, half, outputs)
    return (*outputs, grads)


def local(tokens, grad_out, route_weights, expert_ids, swap_code, w_in, w_down, moment1, moment2):
    expert_count = lax.axis_size("expert")
    sections = expert_count.bit_length() - 1
    columns = max(1, expert_count // 2)
    axis_sizes = (lax.axis_size("dp") // columns, columns)
    chunks = 4
    own_slot = lax.axis_index("expert")
    picked = pick_rows(tokens, grad_out, route_weights, expert_ids, expert_count)

    slots = jnp.arange(expert_count, dtype=jnp.int32)
    order = slots
    for bit in range(sections):
        partner = jnp.bitwise_xor(slots, 1 << bit)
        swapped = swap_code[jnp.minimum(slots, partner)] // (1 << bit) % 2 == 1
        order = order[jnp.where(swapped, partner, slots)]
    source = jnp.sum(jnp.where(slots == own_slot, order, 0))
    operands = (picked, source, w_in, w_down, moment1, moment2)

    free = [(b, s) for b in range(sections) for s in range(1, expert_count) if not s >> b & 1]
    fixed = [(b, 0) for b in range(sections)]
    if len(free) <= 2:
        branches = []
        for taken in itertools.product((False, True), repeat=len(free)):
            pairs = fixed + [pair for pair, yes in zip(free, taken) if yes]
            order_now = static_order(expert_count, sections, pairs)
            move = functools.partial(
                lax.ppermute, axis_name="expert", perm=[(order_now[s], s) for s in range(expert_count)]
            )
            branches.append(functools.partial(layer, move, axis_sizes, sections, chunks))
        which = jnp.int32(0)
        for bit, slot in free:
            which = which * 2 + swap_code[slot] // (1 << bit) % 2
        return lax.switch(which, branches, *operands)

    swaps = section_swaps(swap_code, own_slot, sections)

    def move_by_sections(array):
        for bit in range(sections):
            pairs = [(i, i ^ (1 << bit)) for i in range(expert_count)]
            array = jnp.where(swaps[bit], lax.ppermute(array, "expert", pairs), array)
        return array

    return layer(move_by_sections, axis_sizes, sections, chunks, *operands)


def solution(mesh):
    placed = (
        P(("expert", "dp"), None),
        P(("expert", "dp"), None),
        P(("expert", "dp"), None),
        P(("expert", "dp"), None),
        P(),
        P("expert", None, "dp", None),
        P("expert", "dp", None),
        P("expert", "dp", None),
        P("expert", "dp", None),
    )
    return jax.shard_map(
        local,
        mesh=mesh,
        in_specs=placed,
        out_specs=(
            P("expert", "dp", None),
            P("expert", "dp", None),
            P("expert", "dp", None),
            P("expert", None, "dp", None),
        ),
        check_vma=False,
    )
```

time: 423 us -> 192 us (0.45)
  waiting for transfers between devices: 321 us -> 110 us
  other arithmetic: 37.2 us -> 2.53 us
  starting transfers between devices: 4.65 us -> 35.2 us
  Pallas kernels: 0 us -> 21.7 us
  blocking collectives: 17.8 us -> 0 us
  matrix products: 13.4 us -> 0.66 us
  between operations: 15.6 us -> 5.29 us
    ppermute x8 -> x21, waiting for transfers between devices: 251 us -> 110 us  [the longest x14 97.8 us: shifted(): return lax.ppermute(array, 'dp', pairs)]
    all_gather x2 -> x0, waiting for transfers between devices: 70.4 us -> none  [the longest x1 37.7 us: local(): grad_rows = lax.all_gather(grad_recv, 'dp', axis=0, tiled=True)]
    select_n x11 -> x3, other arithmetic: 32.2 us -> 0.02 us  [the longest x1 0.01 us: local(): order = order[jnp.where(swapped, partner, slots)]]
    ppermute x8 -> x21, starting transfers between devices: 4.57 us -> 35.2 us  [the longest x14 20 us: shifted(): return lax.ppermute(array, 'dp', pairs)]
    pallas_call x0 -> x11, Pallas kernels: none -> 21.7 us  [the longest x4 9.5 us: adam_rows(): pl.pallas_call(functools.partial(adam_kernel, half, chunk), grid=(width /...]
    all_to_all x2 -> x0, blocking collectives: 17.8 us -> none  [the longest x1 9.72 us: local(): lax.all_to_all(tok_send, 'expert', split_axis=0, concat_axis=0, tiled=True)]
    dot_general x6 -> x2, matrix products: 13.4 us -> 0.66 us  [dot(): lax.dot_general(left_side, right_side, (((left_dim,), (right_dim,)), ((),...]
    unnamed x32 -> x8, local copies, waits for them, and re-layouts: 9.36 us -> 3.73 us
  transfers between devices with their start and end apart: 10 -> 21, of which waited for: 7 -> 15; matrix products, arithmetic and copies ran while one was open for 10% -> 2% of each run, Pallas kernels for 0% -> 10%
where the time goes in v1:
time: 192 us
  waiting for transfers between devices  110 us (57%)
  starting transfers between devices  35.2 us (18%)
  Pallas kernels  21.7 us (11%)
  local copies, waits for them, and re-layouts  14.9 us (8%)
  between operations  5.29 us (3%)
  other arithmetic  2.53 us (1%)
    ppermute x14, waiting for transfers between devices, shifted(): return lax.ppermute(array, 'dp', pairs)  97.8 us
    ppermute x14, starting transfers between devices, shifted(): return lax.ppermute(array, 'dp', pairs)  20 us
    ppermute x4, starting transfers between devices, layer(): move(pack(w_down, moment1, moment2, c, chunks))  10.3 us
    pallas_call x4, Pallas kernels, adam_rows(): pl.pallas_call(functools.partial(adam_kernel, half, chunk), grid=(width /...  9.5 us
    ppermute x1, waiting for transfers between devices, layer(): factors = move(factors)  7 us
    ppermute x2, waiting for transfers between devices, exchange(): theirs = lax.ppermute(jnp.concatenate(pieces, axis=0), 'expert', pairs)  5.61 us
    cond x28, local copies, waits for them, and re-layouts  4.87 us
    pallas_call x1, Pallas kernels, grads_of(): pl.pallas_call(functools.partial(grad_kernel, half), grid=(width // tile,...  4.29 us
  transfers between devices with their start and end apart: 21, of which 15 were waited for; matrix products, arithmetic and copies ran while one was open for 2% of the time, Pallas kernels for 10%

profile of v1, /device:TPU:0, one launch (start us, length us, event | category | flops | bytes accessed | tf_op | source)
XLA Modules:
  0.0 191.7 jit_solution(7649820208694660548)
XLA Ops:
  13.9 177.8 %conditional.1 = (bf16[1,256,3584]{2,1,0:T(8,128)(2,1)}, f32[1,256,3584]{2,1,0:T(8,128)}, f32[1,256,3584]{2,1,0:T(8,128)}, bf16[1,2,256,3584]{3,2,1,0:T(8,128)(2,1)}) conditional(s32[]{:T(128)} %clamp.3, (bf16[40,3584]{1,0:T(8,128)(2,1)S(1)}, bf16[1,2,256,3584]{3,2,1,0:T(8,128)(2,1)}, ...), branch_computations={%region_1.2_spmd, %region_2.3_spmd, %region_3.4_spmd, %region_4.5_... | conditional | flops 3618250752 | bytes 198125792 | solution.py:366
  14.0 3.0 %collective-permute-start = (bf16[40,3584]{1,0:T(8,128)(2,1)S(1)}, bf16[40,3584]{1,0:T(8,128)(2,1)}, u32[]{:S(2)}, u32[]{:S(2)}) collective-permute-start(bf16[40,3584]{1,0:T(8,128)(2,1)S(1)} %get-tuple-element.48), channel_id=1, source_target_pairs={{0,16},{8,24},{16,0},{24,8},{1,17},{9,25},{17,1},{25,9},{2,18},{10... | collective-permute-start | bytes 860168 | tf_op jit(solution)/shard_map/cond/branch_0_fun/ppermute | solution.py:309
  18.3 5.6 %collective-permute-done = bf16[40,3584]{1,0:T(8,128)(2,1)} collective-permute-done((bf16[40,3584]{1,0:T(8,128)(2,1)S(1)}, bf16[40,3584]{1,0:T(8,128)(2,1)}, u32[]{:S(2)}, u32[]{:S(2)}) %collective-permute-start) | collective-permute-done | bytes 286752 | tf_op jit(solution)/shard_map/cond/branch_0_fun/ppermute | solution.py:309
  35.9 3.3 %collective-permute-start.19 = (bf16[3,64,3584]{2,1,0:T(8,128)(2,1)S(1)}, bf16[3,64,3584]{2,1,0:T(8,128)(2,1)S(1)}, u32[]{:S(2)}, u32[]{:S(2)}) collective-permute-start(bf16[3,64,3584]{2,1,0:T(8,128)(2,1)S(1)} %pack_state_1.4), channel_id=1, source_target_pairs={{16,0},{0,8},{8,16},{24,24},{17,1},{1,9},{9,17},{25,25},{18,2},{2,... | collective-permute-start | bytes 4128776 | tf_op jit(solution)/shard_map/cond/branch_0_fun/ppermute | solution.py:320
  39.7 2.4 %collective-permute-start.18 = (bf16[3,64,3584]{2,1,0:T(8,128)(2,1)S(1)}, bf16[3,64,3584]{2,1,0:T(8,128)(2,1)S(1)}, u32[]{:S(2)}, u32[]{:S(2)}) collective-permute-start(bf16[3,64,3584]{2,1,0:T(8,128)(2,1)S(1)} %pack_state_2.4), channel_id=1, source_target_pairs={{16,0},{0,8},{8,16},{24,24},{17,1},{1,9},{9,17},{25,25},{18,2},{2,... | collective-permute-start | bytes 4128776 | tf_op jit(solution)/shard_map/cond/branch_0_fun/ppermute | solution.py:320
  45.1 2.7 %collective-permute-start.11 = (bf16[40,3584]{1,0:T(8,128)(2,1)S(1)}, bf16[40,3584]{1,0:T(8,128)(2,1)S(1)}, u32[]{:S(2)}, u32[]{:S(2)}) collective-permute-start(bf16[40,3584]{1,0:T(8,128)(2,1)S(1)} %get-tuple-element.402), channel_id=1, source_target_pairs={{0,4},{1,5},{2,6},{3,7},{4,0},{5,1},{6,2},{7,3},{8,12},{9,13},{10,... | collective-permute-start | bytes 860168 | tf_op jit(solution)/shard_map/cond/branch_0_fun/ppermute | solution.py:261
  47.8 13.8 %collective-permute-done.11 = bf16[40,3584]{1,0:T(8,128)(2,1)S(1)} collective-permute-done((bf16[40,3584]{1,0:T(8,128)(2,1)S(1)}, bf16[40,3584]{1,0:T(8,128)(2,1)S(1)}, u32[]{:S(2)}, u32[]{:S(2)}) %collective-permute-start.11) | collective-permute-done | bytes 286752 | tf_op jit(solution)/shard_map/cond/branch_0_fun/ppermute | solution.py:261
  61.5 2.4 %collective-permute-start.12 = (bf16[40,3584]{1,0:T(8,128)(2,1)S(1)}, bf16[40,3584]{1,0:T(8,128)(2,1)S(1)}, u32[]{:S(2)}, u32[]{:S(2)}) collective-permute-start(bf16[40,3584]{1,0:T(8,128)(2,1)S(1)} %get-tuple-element.402), channel_id=1, source_target_pairs={{0,6},{1,7},{2,0},{3,1},{4,2},{5,3},{6,4},{7,5},{8,14},{9,15},{10,... | collective-permute-start | bytes 860168 | tf_op jit(solution)/shard_map/cond/branch_0_fun/ppermute | solution.py:261
  63.9 6.5 %collective-permute-done.12 = bf16[40,3584]{1,0:T(8,128)(2,1)S(1)} collective-permute-done((bf16[40,3584]{1,0:T(8,128)(2,1)S(1)}, bf16[40,3584]{1,0:T(8,128)(2,1)S(1)}, u32[]{:S(2)}, u32[]{:S(2)}) %collective-permute-start.12) | collective-permute-done | bytes 286752 | tf_op jit(solution)/shard_map/cond/branch_0_fun/ppermute | solution.py:261
  72.0 6.6 %collective-permute-done.13 = bf16[40,3584]{1,0:T(8,128)(2,1)S(1)} collective-permute-done((bf16[40,3584]{1,0:T(8,128)(2,1)S(1)}, bf16[40,3584]{1,0:T(8,128)(2,1)S(1)}, u32[]{:S(2)}, u32[]{:S(2)}) %collective-permute-start.13) | collective-permute-done | bytes 286752 | tf_op jit(solution)/shard_map/cond/branch_0_fun/ppermute | solution.py:261
  78.7 9.4 %collective-permute-done.2 = bf16[40,3584]{1,0:T(8,128)(2,1)S(1)} collective-permute-done((bf16[40,3584]{1,0:T(8,128)(2,1)S(1)}, bf16[40,3584]{1,0:T(8,128)(2,1)S(1)}, u32[]{:S(2)}, u32[]{:S(2)}) %collective-permute-start.2) | collective-permute-done | bytes 286752 | tf_op jit(solution)/shard_map/cond/branch_0_fun/ppermute | solution.py:261
  88.1 12.3 %collective-permute-done.3 = bf16[40,3584]{1,0:T(8,128)(2,1)S(1)} collective-permute-done((bf16[40,3584]{1,0:T(8,128)(2,1)S(1)}, bf16[40,3584]{1,0:T(8,128)(2,1)S(1)}, u32[]{:S(2)}, u32[]{:S(2)}) %collective-permute-start.3) | collective-permute-done | bytes 286752 | tf_op jit(solution)/shard_map/cond/branch_0_fun/ppermute | solution.py:261
  102.8 6.3 %collective-permute-done.4 = bf16[40,3584]{1,0:T(8,128)(2,1)S(1)} collective-permute-done((bf16[40,3584]{1,0:T(8,128)(2,1)S(1)}, bf16[40,3584]{1,0:T(8,128)(2,1)S(1)}, u32[]{:S(2)}, u32[]{:S(2)}) %collective-permute-start.4) | collective-permute-done | bytes 286752 | tf_op jit(solution)/shard_map/cond/branch_0_fun/ppermute | solution.py:261
  110.5 6.5 %collective-permute-done.5 = bf16[40,3584]{1,0:T(8,128)(2,1)S(1)} collective-permute-done((bf16[40,3584]{1,0:T(8,128)(2,1)S(1)}, bf16[40,3584]{1,0:T(8,128)(2,1)S(1)}, u32[]{:S(2)}, u32[]{:S(2)}) %collective-permute-start.5) | collective-permute-done | bytes 286752 | tf_op jit(solution)/shard_map/cond/branch_0_fun/ppermute | solution.py:261
  118.4 5.7 %collective-permute-done.14 = bf16[40,3584]{1,0:T(8,128)(2,1)S(1)} collective-permute-done((bf16[40,3584]{1,0:T(8,128)(2,1)S(1)}, bf16[40,3584]{1,0:T(8,128)(2,1)S(1)}, u32[]{:S(2)}, u32[]{:S(2)}) %collective-permute-start.14) | collective-permute-done | bytes 286752 | tf_op jit(solution)/shard_map/cond/branch_0_fun/ppermute | solution.py:261
  125.4 6.4 %collective-permute-done.15 = bf16[40,3584]{1,0:T(8,128)(2,1)S(1)} collective-permute-done((bf16[40,3584]{1,0:T(8,128)(2,1)S(1)}, bf16[40,3584]{1,0:T(8,128)(2,1)S(1)}, u32[]{:S(2)}, u32[]{:S(2)}) %collective-permute-start.15) | collective-permute-done | bytes 286752 | tf_op jit(solution)/shard_map/cond/branch_0_fun/ppermute | solution.py:261
  133.2 7.6 %collective-permute-done.6 = bf16[40,3584]{1,0:T(8,128)(2,1)S(1)} collective-permute-done((bf16[40,3584]{1,0:T(8,128)(2,1)S(1)}, bf16[40,3584]{1,0:T(8,128)(2,1)S(1)}, u32[]{:S(2)}, u32[]{:S(2)}) %collective-permute-start.6) | collective-permute-done | bytes 286752 | tf_op jit(solution)/shard_map/cond/branch_0_fun/ppermute | solution.py:261
  142.1 8.0 %collective-permute-done.7 = bf16[40,3584]{1,0:T(8,128)(2,1)S(1)} collective-permute-done((bf16[40,3584]{1,0:T(8,128)(2,1)S(1)}, bf16[40,3584]{1,0:T(8,128)(2,1)S(1)}, u32[]{:S(2)}, u32[]{:S(2)}) %collective-permute-start.7) | collective-permute-done | bytes 286752 | tf_op jit(solution)/shard_map/cond/branch_0_fun/ppermute | solution.py:261
  151.4 7.2 %collective-permute-done.8 = bf16[40,3584]{1,0:T(8,128)(2,1)S(1)} collective-permute-done((bf16[40,3584]{1,0:T(8,128)(2,1)S(1)}, bf16[40,3584]{1,0:T(8,128)(2,1)S(1)}, u32[]{:S(2)}, u32[]{:S(2)}) %collective-permute-start.8) | collective-permute-done | bytes 286752 | tf_op jit(solution)/shard_map/cond/branch_0_fun/ppermute | solution.py:261
  160.0 3.9 %factors.4 = bf16[320,512]{1,0:T(8,128)(2,1)S(1)} custom-call(bf16[320,3584]{1,0:T(8,128)(2,1)S(1)} %constant_dynamic-update-slice_fusion.3.x_ref, bf16[1,2,256,3584]{3,2,1,0:T(8,128)(2,1)S(1)} %copy-done.28, bf16[1,256,3584]{2,1,0:T(8,128)(2,1)S(1)} %copy-done.12), custom_call_target="tpu_custom_call" | custom-call | flops 1761607680 | bytes 7798784 | tf_op jit(solution)/shard_map/cond/branch_0_fun/factors/pallas_call | solution.py:139
  167.2 7.0 %collective-permute-done.9.factor_ref = bf16[320,512]{1,0:T(8,128)(2,1)S(1)} collective-permute-done((bf16[320,512]{1,0:T(8,128)(2,1)S(1)}, bf16[320,512]{1,0:T(8,128)(2,1)S(1)}, u32[]{:S(2)}, u32[]{:S(2)}) %collective-permute-start.9) | collective-permute-done | bytes 327712 | tf_op jit(solution)/shard_map/cond/branch_0_fun/ppermute | solution.py:326
  176.6 2.4 %adam_rows_1.4 = (bf16[1,256,3584]{2,1,0:T(8,128)(2,1)S(1)}, f32[1,256,3584]{2,1,0:T(8,128)S(1)}, f32[1,256,3584]{2,1,0:T(8,128)S(1)}) custom-call(bf16[320,512]{1,0:T(8,128)(2,1)S(1)} %collective-permute-done.9.factor_ref, ...), custom_call_target="tpu_custom_call", output_to_operand_aliasing={{0}: (3, {}), {1}: (4, {}), {2}: (5, {})} | custom-call | flops 146800640 | bytes 5963776 | tf_op jit(solution)/shard_map/cond/branch_0_fun/adam_rows_1/pallas_call | solution.py:234
  181.4 4.3 %in_grads.4 = bf16[1,2,256,3584]{3,2,1,0:T(8,128)(2,1)} custom-call(bf16[320,512]{1,0:T(8,128)(2,1)S(1)} %collective-permute-done.9.factor_ref, bf16[320,3584]{1,0:T(8,128)(2,1)S(1)} %constant_dynamic-update-slice_fusion.11.x_ref), custom_call_target="tpu_custom_call" | custom-call | flops 1174405120 | bytes 5963776 | tf_op jit(solution)/shard_map/cond/branch_0_fun/in_grads/pallas_call | solution.py:170
  185.7 2.4 %adam_rows_3.4 = (bf16[1,256,3584]{2,1,0:T(8,128)(2,1)S(1)}, f32[1,256,3584]{2,1,0:T(8,128)S(1)}, f32[1,256,3584]{2,1,0:T(8,128)S(1)}) custom-call(bf16[320,512]{1,0:T(8,128)(2,1)S(1)} %collective-permute-done.9.factor_ref, ...), custom_call_target="tpu_custom_call", output_to_operand_aliasing={{0}: (3, {}), {1}: (4, {}), {2}: (5, {})} | custom-call | flops 146800640 | bytes 5963776 | tf_op jit(solution)/shard_map/cond/branch_0_fun/adam_rows_3/pallas_call | solution.py:234
  (93 shorter events, 49.7 us)
Async XLA Ops:
  14.0 10.0 %collective-permute-start = (bf16[40,3584]{1,0:T(8,128)(2,1)S(1)}, bf16[40,3584]{1,0:T(8,128)(2,1)}, u32[]{:S(2)}, u32[]{:S(2)}) collective-permute-start(bf16[40,3584]{1,0:T(8,128)(2,1)S(1)} %get-tuple-element.48), channel_id=1, source_target_pairs={{0,16},{8,24},{16,0},{24,8},{1,17},{9,25},{17,1},{25,9},{2,18},{10... | collective-permute-start | bytes 860168 | tf_op jit(solution)/shard_map/cond/branch_0_fun/ppermute | solution.py:309
  18.3 13.0 %copy-start.12 = (bf16[1,256,3584]{2,1,0:T(8,128)(2,1)S(1)}, bf16[1,256,3584]{2,1,0:T(8,128)(2,1)}, u32[]{:S(2)}) copy-start(bf16[1,256,3584]{2,1,0:T(8,128)(2,1)} %get-tuple-element.153.w_down_ref.w_ref) | copy-start | bytes 5505028 | tf_op jit(solution)/shard_map/cond
  25.7 2.3 %collective-permute-start.1 = (bf16[80,3584]{1,0:T(8,128)(2,1)}, bf16[80,3584]{1,0:T(8,128)(2,1)}, u32[]{:S(2)}, u32[]{:S(2)}) collective-permute-start(bf16[80,3584]{1,0:T(8,128)(2,1)} %pad_maximum_fusion), channel_id=1, source_target_pairs={{0,8},{8,0},{16,24},{24,16},{1,9},{9,1},{17,25},{25,17},{2,10},{10... | collective-permute-start | bytes 1720328 | tf_op jit(solution)/shard_map/cond/branch_0_fun/ppermute | solution.py:309
  29.5 15.6 %collective-permute-start.10 = (bf16[40,3584]{1,0:T(8,128)(2,1)S(1)}, bf16[40,3584]{1,0:T(8,128)(2,1)S(1)}, u32[]{:S(2)}, u32[]{:S(2)}) collective-permute-start(bf16[40,3584]{1,0:T(8,128)(2,1)S(1)} %get-tuple-element.402), channel_id=1, source_target_pairs={{0,2},{1,3},{2,4},{3,5},{4,6},{5,7},{6,0},{7,1},{8,10},{9,11},{10,... | collective-permute-start | bytes 860168 | tf_op jit(solution)/shard_map/cond/branch_0_fun/ppermute | solution.py:261
  31.3 4.1 %copy-start.8 = (f32[1,256,3584]{2,1,0:T(8,128)S(1)}, f32[1,256,3584]{2,1,0:T(8,128)}, u32[]{:S(2)}) copy-start(f32[1,256,3584]{2,1,0:T(8,128)} %get-tuple-element.173.two_ref) | copy-start | bytes 11010052 | tf_op jit(solution)/shard_map/cond
  33.1 134.2 %collective-permute-start.20 = (bf16[3,64,3584]{2,1,0:T(8,128)(2,1)S(1)}, bf16[3,64,3584]{2,1,0:T(8,128)(2,1)S(1)}, u32[]{:S(2)}, u32[]{:S(2)}) collective-permute-start(bf16[3,64,3584]{2,1,0:T(8,128)(2,1)S(1)} %pack_state_0.4), channel_id=1, source_target_pairs={{16,0},{0,8},{8,16},{24,24},{17,1},{1,9},{9,17},{25,25},{18,2},{2,... | collective-permute-start | bytes 4128776 | tf_op jit(solution)/shard_map/cond/branch_0_fun/ppermute | solution.py:320
  35.9 140.6 %collective-permute-start.19 = (bf16[3,64,3584]{2,1,0:T(8,128)(2,1)S(1)}, bf16[3,64,3584]{2,1,0:T(8,128)(2,1)S(1)}, u32[]{:S(2)}, u32[]{:S(2)}) collective-permute-start(bf16[3,64,3584]{2,1,0:T(8,128)(2,1)S(1)} %pack_state_1.4), channel_id=1, source_target_pairs={{16,0},{0,8},{8,16},{24,24},{17,1},{1,9},{9,17},{25,25},{18,2},{2,... | collective-permute-start | bytes 4128776 | tf_op jit(solution)/shard_map/cond/branch_0_fun/ppermute | solution.py:320
  39.7 139.3 %collective-permute-start.18 = (bf16[3,64,3584]{2,1,0:T(8,128)(2,1)S(1)}, bf16[3,64,3584]{2,1,0:T(8,128)(2,1)S(1)}, u32[]{:S(2)}, u32[]{:S(2)}) collective-permute-start(bf16[3,64,3584]{2,1,0:T(8,128)(2,1)S(1)} %pack_state_2.4), channel_id=1, source_target_pairs={{16,0},{0,8},{8,16},{24,24},{17,1},{1,9},{9,17},{25,25},{18,2},{2,... | collective-permute-start | bytes 4128776 | tf_op jit(solution)/shard_map/cond/branch_0_fun/ppermute | solution.py:320
  42.6 143.1 %collective-permute-start.17 = (bf16[3,64,3584]{2,1,0:T(8,128)(2,1)S(1)}, bf16[3,64,3584]{2,1,0:T(8,128)(2,1)S(1)}, u32[]{:S(2)}, u32[]{:S(2)}) collective-permute-start(bf16[3,64,3584]{2,1,0:T(8,128)(2,1)S(1)} %pack_state_3.4), channel_id=1, source_target_pairs={{16,0},{0,8},{8,16},{24,24},{17,1},{1,9},{9,17},{25,25},{18,2},{2,... | collective-permute-start | bytes 4128776 | tf_op jit(solution)/shard_map/cond/branch_0_fun/ppermute | solution.py:320
  45.1 16.4 %collective-permute-start.11 = (bf16[40,3584]{1,0:T(8,128)(2,1)S(1)}, bf16[40,3584]{1,0:T(8,128)(2,1)S(1)}, u32[]{:S(2)}, u32[]{:S(2)}) collective-permute-start(bf16[40,3584]{1,0:T(8,128)(2,1)S(1)} %get-tuple-element.402), channel_id=1, source_target_pairs={{0,4},{1,5},{2,6},{3,7},{4,0},{5,1},{6,2},{7,3},{8,12},{9,13},{10,... | collective-permute-start | bytes 860168 | tf_op jit(solution)/shard_map/cond/branch_0_fun/ppermute | solution.py:261
  61.5 8.9 %collective-permute-start.12 = (bf16[40,3584]{1,0:T(8,128)(2,1)S(1)}, bf16[40,3584]{1,0:T(8,128)(2,1)S(1)}, u32[]{:S(2)}, u32[]{:S(2)}) collective-permute-start(bf16[40,3584]{1,0:T(8,128)(2,1)S(1)} %get-tuple-element.402), channel_id=1, source_target_pairs={{0,6},{1,7},{2,0},{3,1},{4,2},{5,3},{6,4},{7,5},{8,14},{9,15},{10,... | collective-permute-start | bytes 860168 | tf_op jit(solution)/shard_map/cond/branch_0_fun/ppermute | solution.py:261
  70.5 8.1 %collective-permute-start.13 = (bf16[40,3584]{1,0:T(8,128)(2,1)S(1)}, bf16[40,3584]{1,0:T(8,128)(2,1)S(1)}, u32[]{:S(2)}, u32[]{:S(2)}) collective-permute-start(bf16[40,3584]{1,0:T(8,128)(2,1)S(1)} %get-tuple-element.402), channel_id=1, source_target_pairs={{0,1},{1,0},{2,3},{3,2},{4,5},{5,4},{6,7},{7,6},{8,9},{9,8},{10,11... | collective-permute-start | bytes 860168 | tf_op jit(solution)/shard_map/cond/branch_0_fun/ppermute | solution.py:261
  78.6 9.5 %collective-permute-start.2 = (bf16[40,3584]{1,0:T(8,128)(2,1)S(1)}, bf16[40,3584]{1,0:T(8,128)(2,1)S(1)}, u32[]{:S(2)}, u32[]{:S(2)}) collective-permute-start(bf16[40,3584]{1,0:T(8,128)(2,1)S(1)} %get-tuple-element.400), channel_id=1, source_target_pairs={{0,2},{1,3},{2,4},{3,5},{4,6},{5,7},{6,0},{7,1},{8,10},{9,11},{10,... | collective-permute-start | bytes 860168 | tf_op jit(solution)/shard_map/cond/branch_0_fun/ppermute | solution.py:261
  88.1 12.4 %collective-permute-start.3 = (bf16[40,3584]{1,0:T(8,128)(2,1)S(1)}, bf16[40,3584]{1,0:T(8,128)(2,1)S(1)}, u32[]{:S(2)}, u32[]{:S(2)}) collective-permute-start(bf16[40,3584]{1,0:T(8,128)(2,1)S(1)} %get-tuple-element.400), channel_id=1, source_target_pairs={{0,4},{1,5},{2,6},{3,7},{4,0},{5,1},{6,2},{7,3},{8,12},{9,13},{10,... | collective-permute-start | bytes 860168 | tf_op jit(solution)/shard_map/cond/branch_0_fun/ppermute | solution.py:261
  88.1 71.9 %copy-start.28 = (bf16[1,2,256,3584]{3,2,1,0:T(8,128)(2,1)S(1)}, bf16[1,2,256,3584]{3,2,1,0:T(8,128)(2,1)}, u32[]{:S(2)}) copy-start(bf16[1,2,256,3584]{3,2,1,0:T(8,128)(2,1)} %get-tuple-element.149.w_in_ref) | copy-start | bytes 11010052 | tf_op jit(solution)/shard_map/cond
  100.5 8.7 %collective-permute-start.4 = (bf16[40,3584]{1,0:T(8,128)(2,1)S(1)}, bf16[40,3584]{1,0:T(8,128)(2,1)S(1)}, u32[]{:S(2)}, u32[]{:S(2)}) collective-permute-start(bf16[40,3584]{1,0:T(8,128)(2,1)S(1)} %get-tuple-element.400), channel_id=1, source_target_pairs={{0,6},{1,7},{2,0},{3,1},{4,2},{5,3},{6,4},{7,5},{8,14},{9,15},{10,... | collective-permute-start | bytes 860168 | tf_op jit(solution)/shard_map/cond/branch_0_fun/ppermute | solution.py:261
  109.2 7.9 %collective-permute-start.5 = (bf16[40,3584]{1,0:T(8,128)(2,1)S(1)}, bf16[40,3584]{1,0:T(8,128)(2,1)S(1)}, u32[]{:S(2)}, u32[]{:S(2)}) collective-permute-start(bf16[40,3584]{1,0:T(8,128)(2,1)S(1)} %get-tuple-element.400), channel_id=1, source_target_pairs={{0,1},{1,0},{2,3},{3,2},{4,5},{5,4},{6,7},{7,6},{8,9},{9,8},{10,11... | collective-permute-start | bytes 860168 | tf_op jit(solution)/shard_map/cond/branch_0_fun/ppermute | solution.py:261
  117.1 7.0 %collective-permute-start.14 = (bf16[40,3584]{1,0:T(8,128)(2,1)S(1)}, bf16[40,3584]{1,0:T(8,128)(2,1)S(1)}, u32[]{:S(2)}, u32[]{:S(2)}) collective-permute-start(bf16[40,3584]{1,0:T(8,128)(2,1)S(1)} %collective-permute-done.10), channel_id=1, source_target_pairs={{0,1},{1,0},{2,3},{3,2},{4,5},{5,4},{6,7},{7,6},{8,9},{9,8},{10,11... | collective-permute-start | bytes 860168 | tf_op jit(solution)/shard_map/cond/branch_0_fun/ppermute | solution.py:261
  124.1 7.8 %collective-permute-start.15 = (bf16[40,3584]{1,0:T(8,128)(2,1)S(1)}, bf16[40,3584]{1,0:T(8,128)(2,1)S(1)}, u32[]{:S(2)}, u32[]{:S(2)}) collective-permute-start(bf16[40,3584]{1,0:T(8,128)(2,1)S(1)} %collective-permute-done.11), channel_id=1, source_target_pairs={{0,1},{1,0},{2,3},{3,2},{4,5},{5,4},{6,7},{7,6},{8,9},{9,8},{10,11... | collective-permute-start | bytes 860168 | tf_op jit(solution)/shard_map/cond/branch_0_fun/ppermute | solution.py:261
  131.8 8.9 %collective-permute-start.6 = (bf16[40,3584]{1,0:T(8,128)(2,1)S(1)}, bf16[40,3584]{1,0:T(8,128)(2,1)S(1)}, u32[]{:S(2)}, u32[]{:S(2)}) collective-permute-start(bf16[40,3584]{1,0:T(8,128)(2,1)S(1)} %collective-permute-done.2), channel_id=1, source_target_pairs={{0,1},{1,0},{2,3},{3,2},{4,5},{5,4},{6,7},{7,6},{8,9},{9,8},{10,11... | collective-permute-start | bytes 860168 | tf_op jit(solution)/shard_map/cond/branch_0_fun/ppermute | solution.py:261
  140.8 9.3 %collective-permute-start.7 = (bf16[40,3584]{1,0:T(8,128)(2,1)S(1)}, bf16[40,3584]{1,0:T(8,128)(2,1)S(1)}, u32[]{:S(2)}, u32[]{:S(2)}) collective-permute-start(bf16[40,3584]{1,0:T(8,128)(2,1)S(1)} %collective-permute-done.3), channel_id=1, source_target_pairs={{0,1},{1,0},{2,3},{3,2},{4,5},{5,4},{6,7},{7,6},{8,9},{9,8},{10,11... | collective-permute-start | bytes 860168 | tf_op jit(solution)/shard_map/cond/branch_0_fun/ppermute | solution.py:261
  150.1 8.6 %collective-permute-start.8 = (bf16[40,3584]{1,0:T(8,128)(2,1)S(1)}, bf16[40,3584]{1,0:T(8,128)(2,1)S(1)}, u32[]{:S(2)}, u32[]{:S(2)}) collective-permute-start(bf16[40,3584]{1,0:T(8,128)(2,1)S(1)} %collective-permute-done.4), channel_id=1, source_target_pairs={{0,1},{1,0},{2,3},{3,2},{4,5},{5,4},{6,7},{7,6},{8,9},{9,8},{10,11... | collective-permute-start | bytes 860168 | tf_op jit(solution)/shard_map/cond/branch_0_fun/ppermute | solution.py:261
  158.7 6.6 %collective-permute-start.16 = (bf16[40,3584]{1,0:T(8,128)(2,1)S(1)}, bf16[40,3584]{1,0:T(8,128)(2,1)S(1)}, u32[]{:S(2)}, u32[]{:S(2)}) collective-permute-start(bf16[40,3584]{1,0:T(8,128)(2,1)S(1)} %collective-permute-done.12), channel_id=1, source_target_pairs={{0,1},{1,0},{2,3},{3,2},{4,5},{5,4},{6,7},{7,6},{8,9},{9,8},{10,11... | collective-permute-start | bytes 860168 | tf_op jit(solution)/shard_map/cond/branch_0_fun/ppermute | solution.py:261
  165.3 9.0 %collective-permute-start.9 = (bf16[320,512]{1,0:T(8,128)(2,1)S(1)}, bf16[320,512]{1,0:T(8,128)(2,1)S(1)}, u32[]{:S(2)}, u32[]{:S(2)}) collective-permute-start(bf16[320,512]{1,0:T(8,128)(2,1)S(1)} %factors.4), channel_id=1, source_target_pairs={{16,0},{0,8},{8,16},{24,24},{17,1},{1,9},{9,17},{25,25},{18,2},{2,... | collective-permute-start | bytes 983048 | tf_op jit(solution)/shard_map/cond/branch_0_fun/ppermute | solution.py:326
  (8 other events, 16.4 us)

commit v2 on v0

v2 whole, which is shorter than its diff:
```python
import functools
import itertools

import jax
import jax.numpy as jnp
from jax import lax
from jax.experimental import pallas as pl
from jax.experimental.pallas import tpu as pltpu
from jax.sharding import PartitionSpec as P

CAP = 5
PIECE = 24
VMEM_LIMIT = 60 * 1024 * 1024

adam_rate = 0.01
beta_one = 0.9
beta_two = 0.999
adam_step = 100.0
adam_eps = 1e-08


def dot(left_side, right_side, left_dim, right_dim):
    return lax.dot_general(
        left_side,
        right_side,
        (((left_dim,), (right_dim,)), ((), ())),
        preferred_element_type=jnp.float32,
    )


def params(limit=VMEM_LIMIT):
    return pltpu.CompilerParams(vmem_limit_bytes=limit)


def cost(flops, nbytes):
    return pl.CostEstimate(flops=int(flops), bytes_accessed=int(nbytes), transcendentals=0)


def tile_of(width, most):
    tile = 128
    for count in range(1, width // 128 + 1):
        if width % (count * 128) == 0 and count * 128 <= most:
            tile = count * 128
    return tile


def pick_kernel(order, pieces, *refs):
    if order is None:
        order, refs = [refs[0][s] for s in range(pieces)], refs[1:]
    ids_ref, weights_ref, tok_ref, grad_ref = refs[:4]
    outs, (sel, scale) = refs[4 : 4 + pieces], refs[4 + pieces :]
    rows = tok_ref.shape[0]
    own_slot = lax.axis_index("expert")

    @pl.when(pl.program_id(0) == 0)
    def _():
        ids = ids_ref[...]
        weights = weights_ref[...]
        earlier = (
            lax.broadcasted_iota(jnp.int32, (rows, rows), 0)
            < lax.broadcasted_iota(jnp.int32, (rows, rows), 1)
        ).astype(jnp.bfloat16)
        want_count = 2 * pieces
        place = lax.broadcasted_iota(jnp.int32, (want_count, rows), 0)
        hits = jnp.zeros((want_count, rows), jnp.float32)
        shares = []
        for piece in range(pieces):
            slot = jnp.bitwise_xor(own_slot, piece)
            source = jnp.int32(0)
            for target in range(pieces):
                source = jnp.where(slot == target, order[target], source)
            for role, expert in enumerate((slot, source)):
                named = ids == expert
                hit = jnp.max(jnp.where(named, 1.0, 0.0), axis=0, keepdims=True)
                hits = jnp.where(place == 2 * piece + role, hit, hits)
                shares.append(jnp.sum(jnp.where(named, weights, 0.0), axis=0, keepdims=True))
        ranks = dot(hits.astype(jnp.bfloat16), earlier, 1, 0)
        ranks = jnp.where(hits > 0.0, ranks, -1.0).astype(jnp.int32)
        row = lax.broadcasted_iota(jnp.int32, (PIECE, rows), 0)
        of_role = jnp.where(row >= 2 * CAP, row - 2 * CAP, row)
        is_grad = of_role >= CAP
        copy = jnp.where(is_grad, of_role - CAP, of_role)
        for piece in range(pieces):
            first, second = 2 * piece, 2 * piece + 1
            is_first = row < 2 * CAP
            rank = jnp.where(is_first, ranks[first : first + 1], ranks[second : second + 1])
            share = jnp.where(is_first, shares[first], shares[second])
            match = jnp.logical_and(copy == rank, row < 4 * CAP)
            part = pl.ds(piece * PIECE, PIECE)
            sel[0, part] = jnp.where(jnp.logical_and(match, jnp.logical_not(is_grad)), 1.0, 0.0)
            sel[1, part] = jnp.where(jnp.logical_and(match, is_grad), 1.0, 0.0)
            scale[part] = jnp.sum(jnp.where(match, share, 0.0), axis=1, keepdims=True)

    token_part = dot(sel[0].astype(jnp.bfloat16), tok_ref[...], 1, 0)
    grad_part = dot(sel[1].astype(jnp.bfloat16), grad_ref[...], 1, 0)
    picked = token_part + scale[...] * grad_part
    for piece in range(pieces):
        outs[piece][...] = picked[piece * PIECE : (piece + 1) * PIECE].astype(jnp.bfloat16)


def pick_rows(order, tokens, grad_out, route_weights, expert_ids):
    pieces = len(order)
    rows, width = tokens.shape
    top = expert_ids.shape[1]
    total = pieces * PIECE
    tile = tile_of(width, 1792)
    known = all(isinstance(s, int) for s in order)
    return pl.pallas_call(
        functools.partial(pick_kernel, tuple(order) if known else None, pieces),
        grid_spec=pltpu.PrefetchScalarGridSpec(
            num_scalar_prefetch=0 if known else 1,
            grid=(width // tile,),
            in_specs=[
                pl.BlockSpec((top, rows), lambda j, *_: (0, 0)),
                pl.BlockSpec((top, rows), lambda j, *_: (0, 0)),
                pl.BlockSpec((rows, tile), lambda j, *_: (0, j)),
                pl.BlockSpec((rows, tile), lambda j, *_: (0, j)),
            ],
            out_specs=[pl.BlockSpec((PIECE, tile), lambda j, *_: (0, j))] * pieces,
            scratch_shapes=[
                pltpu.VMEM((2, total, rows), jnp.float32),
                pltpu.VMEM((total, 1), jnp.float32),
            ],
        ),
        out_shape=[jax.ShapeDtypeStruct((PIECE, width), jnp.bfloat16)] * pieces,
        compiler_params=params(),
        cost_estimate=cost(4 * total * rows * width, 4 * rows * width),
        name="pick_rows",
    )(*(() if known else (jnp.stack(order),)), expert_ids.T, route_weights.T, tokens, grad_out)


def join_kernel(pieces, *refs):
    ins, (own_ref, new_ref) = refs[:pieces], refs[pieces:]
    half = pieces * CAP
    own_slot = lax.axis_index("expert")
    shape = (4 * half, pieces * PIECE)
    row = lax.broadcasted_iota(jnp.int32, shape, 0)
    column = lax.broadcasted_iota(jnp.int32, shape, 1)
    is_second = row >= 2 * half
    of_role = jnp.where(is_second, row - 2 * half, row)
    is_grad = of_role >= half
    in_half = jnp.where(is_grad, of_role - half, of_role)
    chosen = jnp.zeros(shape, jnp.float32)
    for mask in range(pieces):
        copy = in_half - jnp.bitwise_xor(own_slot, mask) * CAP
        wanted = copy + jnp.where(is_grad, CAP, 0) + jnp.where(is_second, 2 * CAP, 0) + mask * PIECE
        mine = jnp.logical_and(copy >= 0, copy < CAP)
        chosen = chosen + jnp.where(jnp.logical_and(mine, column == wanted), 1.0, 0.0)
    rows = jnp.concatenate([ref[...] for ref in ins], axis=0)
    both = dot(chosen.astype(jnp.bfloat16), rows, 1, 0)
    own_ref[...] = both[: 2 * half].astype(jnp.bfloat16)
    new_ref[...] = both[2 * half :].astype(jnp.bfloat16)


def join_pieces(arrays):
    pieces, width = len(arrays), arrays[0].shape[1]
    total = 2 * pieces * CAP
    tile = tile_of(width, 1792)
    return pl.pallas_call(
        functools.partial(join_kernel, pieces),
        grid=(width // tile,),
        in_specs=[pl.BlockSpec((PIECE, tile), lambda j: (0, j))] * pieces,
        out_specs=[pl.BlockSpec((total, tile), lambda j: (0, j))] * 2,
        out_shape=[jax.ShapeDtypeStruct((total, width), jnp.bfloat16)] * 2,
        compiler_params=params(),
        cost_estimate=cost(4 * total * PIECE * pieces * width, 8 * total * width),
        name="join_pieces",
    )(*arrays)


def joined(refs):
    return refs[0][...] if len(refs) == 1 else jnp.concatenate([ref[...] for ref in refs], axis=0)


def parts_spec(parts, tile):
    return [pl.BlockSpec((part.shape[0], tile), lambda j: (0, j)) for part in parts]


def factor_kernel(half, *refs):
    (w_in_ref, w_down_ref, out_ref, acc), x_refs = refs[-4:], refs[:-4]
    step = pl.program_id(0)
    count, units = acc.shape[0], w_down_ref.shape[1]

    @pl.when(step == 0)
    def _():
        acc[...] = jnp.zeros_like(acc)

    x = joined(x_refs)
    acc[:, 0:units] += dot(x, w_in_ref[0, 0], 1, 1)
    acc[:, units : 2 * units] += dot(x, w_in_ref[0, 1], 1, 1)
    acc[:, 2 * units : 3 * units] += dot(x, w_down_ref[0], 1, 1)

    @pl.when(step == pl.num_programs(0) - 1)
    def _():
        gate = acc[:, 0:units]
        up = acc[:, units : 2 * units]
        back = pltpu.roll(acc[:, 2 * units : 3 * units], count - half, 0)
        sig = jax.nn.sigmoid(gate)
        activated = gate * sig
        slopes = sig * (1.0 + gate * (1.0 - sig))
        hidden = pltpu.roll(activated * up, half, 0)
        is_token = lax.broadcasted_iota(jnp.int32, (count, units), 0) % (2 * half) < half
        out_ref[:, 0:units] = jnp.where(is_token, back * up * slopes, hidden).astype(jnp.bfloat16)
        out_ref[:, units : 2 * units] = jnp.where(is_token, back * activated, 0.0).astype(jnp.bfloat16)


def factors_of(parts, w_in, w_down, half):
    count, width = sum(part.shape[0] for part in parts), parts[0].shape[1]
    units = w_down.shape[1]
    tile = tile_of(width, 896)
    return pl.pallas_call(
        functools.partial(factor_kernel, half),
        grid=(width // tile,),
        in_specs=[
            *parts_spec(parts, tile),
            pl.BlockSpec((1, 2, units, tile), lambda j: (0, 0, 0, j)),
            pl.BlockSpec((1, units, tile), lambda j: (0, 0, j)),
        ],
        out_specs=pl.BlockSpec((count, 2 * units), lambda j: (0, 0)),
        out_shape=jax.ShapeDtypeStruct((count, 2 * units), jnp.bfloat16),
        scratch_shapes=[pltpu.VMEM((count, 3 * units), jnp.float32)],
        compiler_params=params(),
        cost_estimate=cost(6 * count * units * width, 6 * units * width + 2 * count * width),
        name="factors",
    )(*parts, w_in, w_down)


def new_rows_of(crossing, x_refs):
    if crossing is None:
        return joined(x_refs)
    own_slot = lax.axis_index("expert")
    gathered = functools.reduce(jnp.logical_or, [own_slot == slot for slot in crossing])
    return jnp.where(gathered, joined(x_refs[:-1]), x_refs[-1][...])


def grad_kernel(half, crossing, factor_ref, *refs):
    (out_ref, turned), x_refs = refs[-2:], refs[:-2]
    units = out_ref.shape[2]

    @pl.when(pl.program_id(0) == 0)
    def _():
        is_token = lax.broadcasted_iota(jnp.int32, factor_ref.shape, 0) % (2 * half) < half
        both = factor_ref[...].astype(jnp.float32)
        turned[...] = jnp.where(is_token, both, 0.0).T.astype(jnp.bfloat16)

    grads = dot(turned[...], new_rows_of(crossing, x_refs), 1, 0)
    out_ref[0, 0] = grads[:units].astype(jnp.bfloat16)
    out_ref[0, 1] = grads[units:].astype(jnp.bfloat16)


def grads_of(factors, crossing, parts, half):
    count, width = factors.shape[0], parts[0].shape[1]
    units = factors.shape[1] // 2
    tile = tile_of(width, 896)
    return pl.pallas_call(
        functools.partial(grad_kernel, half, crossing),
        grid=(width // tile,),
        in_specs=[
            pl.BlockSpec((count, 2 * units), lambda j: (0, 0)),
            *parts_spec(parts, tile),
        ],
        out_specs=pl.BlockSpec((1, 2, units, tile), lambda j: (0, 0, 0, j)),
        out_shape=jax.ShapeDtypeStruct((1, 2, units, width), jnp.bfloat16),
        scratch_shapes=[pltpu.VMEM((2 * units, count), jnp.bfloat16)],
        compiler_params=params(),
        cost_estimate=cost(4 * count * units * width, 4 * units * width + 2 * count * width),
        name="in_grads",
    )(factors, *parts)


def pack_kernel(*refs):
    for number, ref in enumerate(refs[:-1]):
        refs[-1][number] = ref[0].astype(jnp.bfloat16)


def pack(*arrays):
    _, units, width = arrays[0].shape
    count = len(arrays)
    tile = tile_of(width, 896)
    return pl.pallas_call(
        pack_kernel,
        grid=(width // tile,),
        in_specs=[pl.BlockSpec((1, units, tile), lambda j: (0, 0, j))] * count,
        out_specs=pl.BlockSpec((count, units, tile), lambda j: (0, 0, j)),
        out_shape=jax.ShapeDtypeStruct((count, units, width), jnp.bfloat16),
        compiler_params=params(),
        cost_estimate=cost(2 * units * width, 16 * units * width),
        name="pack_state",
    )(*arrays)


def adam_kernel(half, crossing, factor_ref, state_ref, *refs):
    (down_ref, one_ref, two_ref, turned), x_refs = refs[-4:], refs[:-4]
    count, units = factor_ref.shape[0], down_ref.shape[1]

    @pl.when(pl.program_id(0) == 0)
    def _():
        is_token = lax.broadcasted_iota(jnp.int32, (count, units), 0) % (2 * half) < half
        both = factor_ref[:, :units].astype(jnp.float32)
        turned[...] = jnp.where(is_token, 0.0, both).T.astype(jnp.bfloat16)

    down_grad = dot(turned[...], new_rows_of(crossing, x_refs), 1, 0)
    w_down, moment1, moment2 = [state_ref[k].astype(jnp.float32) for k in range(3)]
    rate = adam_rate / (1.0 - beta_one**adam_step)
    fix_two = 1.0 / (1.0 - beta_two**adam_step)
    first_new = beta_one * moment1 + (1.0 - beta_one) * down_grad
    second_new = beta_two * moment2 + (1.0 - beta_two) * (down_grad * down_grad)
    change = rate * first_new / (jnp.sqrt(second_new * fix_two) + adam_eps)
    down_ref[0] = (w_down - change).astype(jnp.bfloat16)
    one_ref[0] = first_new
    two_ref[0] = second_new


def adam(factors, crossing, parts, state, half):
    count = factors.shape[0]
    _, units, width = state.shape
    tile = tile_of(width, 512)
    spec = pl.BlockSpec((1, units, tile), lambda j: (0, 0, j))
    return pl.pallas_call(
        functools.partial(adam_kernel, half, crossing),
        grid=(width // tile,),
        in_specs=[
            pl.BlockSpec((count, 2 * units), lambda j: (0, 0)),
            pl.BlockSpec((3, units, tile), lambda j: (0, 0, j)),
            *parts_spec(parts, tile),
        ],
        out_specs=[spec, spec, spec],
        out_shape=[
            jax.ShapeDtypeStruct((1, units, width), kind) for kind in (jnp.bfloat16, jnp.float32, jnp.float32)
        ],
        scratch_shapes=[pltpu.VMEM((units, count), jnp.bfloat16)],
        compiler_params=params(),
        cost_estimate=cost(2 * count * units * width, 16 * units * width + 2 * count * width),
        name="adam",
    )(factors, state, *parts)


def gather_dp(block, columns, slots=None):
    size = lax.axis_size("dp")
    planes = size // columns

    def crossed(array, mask):
        if slots is None:
            return lax.ppermute(array, "dp", [(i, i ^ mask) for i in range(size)])
        pairs = [(s * size + i, s * size + (i ^ mask)) for s in slots for i in range(size)]
        return lax.ppermute(array, ("expert", "dp"), pairs)

    blocks = [block] + [crossed(block, k * columns) for k in range(1, planes)]
    near = jnp.concatenate(blocks[: planes // 2], axis=0)
    far = jnp.concatenate(blocks[planes // 2 :], axis=0)
    return [near, far] + [crossed(p, k) for k in range(1, columns) for p in (near, far)]


def after(array, *others):
    return lax.optimization_barrier((array, *others))[0]


def section_swaps(swap_code, slot, sections):
    swaps = []
    for bit in range(sections):
        lower = jnp.minimum(slot, jnp.bitwise_xor(slot, 1 << bit))
        swaps.append(swap_code[lower] // (1 << bit) % 2 == 1)
    return swaps


def static_order(expert_count, sections, swapped_pairs):
    order = list(range(expert_count))
    for bit in range(sections):
        step = [s ^ (1 << bit) if (bit, min(s, s ^ (1 << bit))) in swapped_pairs else s for s in range(expert_count)]
        order = [order[s] for s in step]
    return order


def layer(move, columns, order, operands):
    tokens, grad_out, route_weights, expert_ids, w_in, w_down, moment1, moment2 = operands
    expert_count = len(order)
    half = expert_count * CAP
    crossing = None
    if all(isinstance(slot, int) for slot in order):
        crossing = [s for s in range(expert_count) if order[s] not in (s, s ^ 1)]
    if crossing is not None and len(crossing) == expert_count:
        crossing = None

    picked = pick_rows(order, tokens, grad_out, route_weights, expert_ids)
    arrived = [picked[0]]
    for mask in range(1, expert_count):
        pairs = [(i, i ^ mask) for i in range(expert_count)]
        arrived.append(lax.ppermute(picked[mask], "expert", pairs))
    state = move(pack(after(w_down, picked[0]), moment1, moment2))
    own_block, new_block = join_pieces(arrived)
    own_parts = gather_dp(own_block, columns)
    factors = factors_of(own_parts, w_in, w_down, half)
    new_parts = gather_dp(after(new_block, *own_parts[:2]), columns, crossing)
    if crossing is not None:
        pairs = [(order[s], s) for s in range(expert_count) if s not in crossing]
        new_parts.append(lax.ppermute(jnp.concatenate(own_parts, axis=0), "expert", pairs))
    factors = move(factors)
    grads = grads_of(factors, crossing, new_parts, half)
    return (*adam(factors, crossing, new_parts, state, half), grads)


def local(tokens, grad_out, route_weights, expert_ids, swap_code, w_in, w_down, moment1, moment2):
    expert_count = lax.axis_size("expert")
    sections = expert_count.bit_length() - 1
    columns = max(1, expert_count // 2)
    operands = (tokens, grad_out, route_weights, expert_ids, w_in, w_down, moment1, moment2)

    free = [(b, s) for b in range(sections) for s in range(1, expert_count) if not s >> b & 1]
    fixed = [(b, 0) for b in range(sections)]
    if len(free) <= 2:
        branches = []
        for taken in itertools.product((False, True), repeat=len(free)):
            pairs = fixed + [pair for pair, yes in zip(free, taken) if yes]
            order = static_order(expert_count, sections, pairs)
            move = functools.partial(
                lax.ppermute, axis_name="expert", perm=[(order[s], s) for s in range(expert_count)]
            )
            branches.append(functools.partial(layer, move, columns, order))
        which = jnp.int32(0)
        for bit, slot in free:
            which = which * 2 + ((swap_code[slot] >> bit) & 1)
        return lax.switch(which, branches, operands)

    swaps = section_swaps(swap_code, lax.axis_index("expert"), sections)

    def move_by_sections(array):
        for bit in range(sections):
            pairs = [(i, i ^ (1 << bit)) for i in range(expert_count)]
            array = jnp.where(swaps[bit], lax.ppermute(array, "expert", pairs), array)
        return array

    slots = jnp.arange(expert_count, dtype=jnp.int32)
    order = slots
    for bit in range(sections):
        partner = jnp.bitwise_xor(slots, 1 << bit)
        swapped = swap_code[jnp.minimum(slots, partner)] // (1 << bit) % 2 == 1
        order = order[jnp.where(swapped, partner, slots)]
    return layer(move_by_sections, columns, [order[s] for s in range(expert_count)], operands)


def solution(mesh):
    placed = (
        P(("expert", "dp"), None),
        P(("expert", "dp"), None),
        P(("expert", "dp"), None),
        P(("expert", "dp"), None),
        P(),
        P("expert", None, "dp", None),
        P("expert", "dp", None),
        P("expert", "dp", None),
        P("expert", "dp", None),
    )
    return jax.shard_map(
        local,
        mesh=mesh,
        in_specs=placed,
        out_specs=(
            P("expert", "dp", None),
            P("expert", "dp", None),
            P("expert", "dp", None),
            P("expert", None, "dp", None),
        ),
        check_vma=False,
    )
```

time: 423 us -> 252 us (0.60)
  waiting for transfers between devices: 321 us -> 189 us
  other arithmetic: 37.2 us -> 0 us
  Pallas kernels: 0 us -> 35.1 us
  blocking collectives: 17.8 us -> 0 us
  starting transfers between devices: 4.65 us -> 18.5 us
  between operations: 15.6 us -> 2.13 us
  matrix products: 13.4 us -> 0 us
  local copies, waits for them, and re-layouts: 12.1 us -> 5.55 us
    all_gather x2 -> x0, waiting for transfers between devices: 70.4 us -> none  [the longest x1 37.7 us: local(): grad_rows = lax.all_gather(grad_recv, 'dp', axis=0, tiled=True)]
    ppermute x8 -> x15, waiting for transfers between devices: 251 us -> 189 us  [the longest x3 125 us: layer(): arrived.append(lax.ppermute(picked[mask], 'expert', pairs))]
    pallas_call x0 -> x6, Pallas kernels: none -> 35.1 us  [the longest x1 11.6 us: adam(): pl.pallas_call(functools.partial(adam_kernel, half, crossing), grid=(widt...]
    select_n x11 -> x0, other arithmetic: 32.2 us -> none  [the longest x8 32.1 us: local(): jnp.where(swapped, theirs, own_part)]
    all_to_all x2 -> x0, blocking collectives: 17.8 us -> none  [the longest x1 9.72 us: local(): lax.all_to_all(tok_send, 'expert', split_axis=0, concat_axis=0, tiled=True)]
    ppermute x8 -> x15, starting transfers between devices: 4.57 us -> 18.5 us  [the longest x10 13.9 us: crossed(): return lax.ppermute(array, 'dp', [(i, i ^ mask) for i in range(size)])]
    dot_general x6 -> x0, matrix products: 13.4 us -> none  [contract(): lax.dot_general(left_side, right_side, (((left_dim,), (right_dim,)), ((),...]
    unnamed x32 -> x0, local copies, waits for them, and re-layouts: 9.36 us -> none
  transfers between devices with their start and end apart: 10 -> 15, of which waited for: 7 -> 8; matrix products, arithmetic and copies ran while one was open for 10% -> 0% of each run, Pallas kernels for 0% -> 6%
where the time goes in v2:
time: 252 us; the launch traced here: 251 us
  waiting for transfers between devices  189 us (75%)
  Pallas kernels  35.1 us (14%)
  starting transfers between devices  18.5 us (7%)
  local copies, waits for them, and re-layouts  5.55 us (2%)
    ppermute x3, waiting for transfers between devices, layer(): arrived.append(lax.ppermute(picked[mask], 'expert', pairs))  125 us
    ppermute x10, waiting for transfers between devices, crossed(): return lax.ppermute(array, 'dp', [(i, i ^ mask) for i in range(size)])  65 us
    ppermute x10, starting transfers between devices, crossed(): return lax.ppermute(array, 'dp', [(i, i ^ mask) for i in range(size)])  13.9 us
    pallas_call x1, Pallas kernels, adam(): pl.pallas_call(functools.partial(adam_kernel, half, crossing), grid=(widt...  11.6 us
    pallas_call x1, Pallas kernels, factors_of(): pl.pallas_call(functools.partial(factor_kernel, half), grid=(width // til...  6.25 us
    pallas_call x1, Pallas kernels, pack(): pl.pallas_call(pack_kernel, grid=(width // tile,), in_specs=[pl.BlockSpec...  6.1 us
    pallas_call x1, Pallas kernels, grads_of(): pl.pallas_call(functools.partial(grad_kernel, half, crossing), grid=(widt...  5.92 us
  transfers between devices with their start and end apart: 15, of which 8 were waited for; matrix products, arithmetic and copies ran while one was open for 0% of the time, Pallas kernels for 6%

profile of v2, /device:TPU:0, one launch (start us, length us, event | category | flops | bytes accessed | tf_op | source)
XLA Modules:
  0.0 251.0 jit_solution(11860904565782318851)
XLA Ops:
  0.6 1.3 fusion
  3.2 247.5 %conditional.1 = (bf16[1,256,3584]{2,1,0:T(8,128)(2,1)}, f32[1,256,3584]{2,1,0:T(8,128)}, f32[1,256,3584]{2,1,0:T(8,128)}, bf16[1,2,256,3584]{3,2,1,0:T(8,128)(2,1)}) conditional(s32[]{:T(128)} %bitcast.8, (s32[128,8]{0,1:T(8,128)}, f32[128,8]{0,1:T(8,128)}, bf16[128,3584]{1,0:T(8,128)(2,1)}, ...), branch_computations={%region_0.0_spmd, %region_1.0_spmd, %region_2.0_spmd, %region_3.0_... | conditional | flops 3756261376 | bytes 137266144 | solution.py:422
  3.3 3.0 %pick_rows.5 = (bf16[24,3584]{1,0:T(8,128)(2,1)}, bf16[24,3584]{1,0:T(8,128)(2,1)}, bf16[24,3584]{1,0:T(8,128)(2,1)}, bf16[24,3584]{1,0:T(8,128)(2,1)}) custom-call(s32[8,128]{1,0:T(8,128)} %bitcast.10, f32[8,128]{1,0:T(8,128)} %bitcast.14, bf16[128,3584]{1,0:T(8,128)(2,1)} %get-tuple-element.85.refs_2_, bf16[128,3584]{1,0:T(8,128)(2,1)} %get-tuple-element.86.refs_3_), custom_call_target="tpu_custom_call" | custom-call | flops 176160768 | bytes 1835008 | tf_op jit(solution)/shard_map/cond/branch_1_fun/pick_rows/pallas_call | solution.py:108
  6.3 6.1 %pack_state.5 = bf16[3,256,3584]{2,1,0:T(8,128)(2,1)} custom-call(bf16[1,256,3584]{2,1,0:T(8,128)(2,1)S(1)} %copy-done.1, f32[1,256,3584]{2,1,0:T(8,128)} %get-tuple-element.95.refs_1_, f32[1,256,3584]{2,1,0:T(8,128)} %get-tuple-element.96.refs_2_), custom_call_target="tpu_custom_call" | custom-call | flops 1835008 | bytes 14680064 | tf_op jit(solution)/shard_map/cond/branch_1_fun/pack_state/pallas_call | solution.py:280
  12.4 2.4 collective-permute-start.25
  15.5 1.4 collective-permute-start.18
  16.9 121.8 %collective-permute-done.17.refs_2_ = bf16[24,3584]{1,0:T(8,128)(2,1)S(1)} collective-permute-done((bf16[24,3584]{1,0:T(8,128)(2,1)S(1)}, bf16[24,3584]{1,0:T(8,128)(2,1)S(1)}, u32[]{:S(2)}, u32[]{:S(2)}) %collective-permute-start.17) | collective-permute-done | bytes 172064 | tf_op jit(solution)/shard_map/cond/branch_1_fun/ppermute | solution.py:388
  138.7 2.7 %collective-permute-done.18.refs_3_ = bf16[24,3584]{1,0:T(8,128)(2,1)S(1)} collective-permute-done((bf16[24,3584]{1,0:T(8,128)(2,1)S(1)}, bf16[24,3584]{1,0:T(8,128)(2,1)S(1)}, u32[]{:S(2)}, u32[]{:S(2)}) %collective-permute-start.18) | collective-permute-done | bytes 172064 | tf_op jit(solution)/shard_map/cond/branch_1_fun/ppermute | solution.py:388
  142.1 2.3 join_pieces.5
  144.4 3.6 %collective-permute-start.21 = (bf16[40,3584]{1,0:T(8,128)(2,1)}, bf16[40,3584]{1,0:T(8,128)(2,1)S(1)}, u32[]{:S(2)}, u32[]{:S(2)}) collective-permute-start(bf16[40,3584]{1,0:T(8,128)(2,1)} %get-tuple-element.91), channel_id=1, source_target_pairs={{0,6},{1,7},{2,4},{3,5},{4,2},{5,3},{6,0},{7,1},{8,14},{9,15},{10,... | collective-permute-start | bytes 860168 | tf_op jit(solution)/shard_map/cond/branch_1_fun/ppermute | solution.py:344
  149.8 23.2 %collective-permute-done.20 = bf16[40,3584]{1,0:T(8,128)(2,1)S(1)} collective-permute-done((bf16[40,3584]{1,0:T(8,128)(2,1)}, bf16[40,3584]{1,0:T(8,128)(2,1)S(1)}, u32[]{:S(2)}, u32[]{:S(2)}) %collective-permute-start.20) | collective-permute-done | bytes 286752 | tf_op jit(solution)/shard_map/cond/branch_1_fun/ppermute | solution.py:344
  173.2 2.5 %collective-permute-start.28 = (bf16[40,3584]{1,0:T(8,128)(2,1)S(1)}, bf16[40,3584]{1,0:T(8,128)(2,1)S(1)}, u32[]{:S(2)}, u32[]{:S(2)}) collective-permute-start(bf16[40,3584]{1,0:T(8,128)(2,1)S(1)} %copy-done.36), channel_id=1, source_target_pairs={{0,6},{1,7},{2,4},{3,5},{4,2},{5,3},{6,0},{7,1},{8,14},{9,15},{10,... | collective-permute-start | bytes 860168 | tf_op jit(solution)/shard_map/cond/branch_1_fun/ppermute | solution.py:344
  175.7 1.9 collective-permute-start.26
  177.6 1.5 collective-permute-start.22
  179.1 14.6 %collective-permute-done.26 = bf16[40,3584]{1,0:T(8,128)(2,1)S(1)} collective-permute-done((bf16[40,3584]{1,0:T(8,128)(2,1)S(1)}, bf16[40,3584]{1,0:T(8,128)(2,1)S(1)}, u32[]{:S(2)}, u32[]{:S(2)}) %collective-permute-start.26) | collective-permute-done | bytes 286752 | tf_op jit(solution)/shard_map/cond/branch_1_fun/ppermute | solution.py:344
  193.7 1.5 collective-permute-start.23
  195.2 3.7 %collective-permute-done.27 = bf16[40,3584]{1,0:T(8,128)(2,1)S(1)} collective-permute-done((bf16[40,3584]{1,0:T(8,128)(2,1)S(1)}, bf16[40,3584]{1,0:T(8,128)(2,1)S(1)}, u32[]{:S(2)}, u32[]{:S(2)}) %collective-permute-start.27) | collective-permute-done | bytes 286752 | tf_op jit(solution)/shard_map/cond/branch_1_fun/ppermute | solution.py:344
  199.0 1.5 collective-permute-start.29
  201.2 8.5 %collective-permute-done.23.refs_3_ = bf16[80,3584]{1,0:T(8,128)(2,1)S(1)} collective-permute-done((bf16[80,3584]{1,0:T(8,128)(2,1)S(1)}, bf16[80,3584]{1,0:T(8,128)(2,1)S(1)}, u32[]{:S(2)}, u32[]{:S(2)}) %collective-permute-start.23) | collective-permute-done | bytes 573472 | tf_op jit(solution)/shard_map/cond/branch_1_fun/ppermute | solution.py:344
  210.5 6.3 %factors.5 = bf16[320,512]{1,0:T(8,128)(2,1)} custom-call(bf16[80,3584]{1,0:T(8,128)(2,1)} %copy-done.22, bf16[80,3584]{1,0:T(8,128)(2,1)} %copy-done.24, bf16[80,3584]{1,0:T(8,128)(2,1)} %copy-done.30, bf16[80,3584]{1,0:T(8,128)(2,1)} %copy-done.32, bf16[1,2,256,3584]{3,2,1,0:T(8,128)(2,1)} %get-tuple-element.92.refs_4_, bf16[1,256,3584]{2,1,0:T(8,128)(2,1)S(1)} %copy-done.1), custom_call_target="tpu_custom_call" | custom-call | flops 1761607680 | bytes 7798784 | tf_op jit(solution)/shard_map/cond/branch_1_fun/factors/pallas_call | solution.py:211
  216.8 5.1 %collective-permute-done.29.refs_2_ = bf16[80,3584]{1,0:T(8,128)(2,1)S(1)} collective-permute-done((bf16[80,3584]{1,0:T(8,128)(2,1)S(1)}, bf16[80,3584]{1,0:T(8,128)(2,1)S(1)}, u32[]{:S(2)}, u32[]{:S(2)}) %collective-permute-start.29) | collective-permute-done | bytes 573472 | tf_op jit(solution)/shard_map/cond/branch_1_fun/ppermute | solution.py:344
  221.9 9.8 %collective-permute-done.30.refs_3_ = bf16[80,3584]{1,0:T(8,128)(2,1)S(1)} collective-permute-done((bf16[80,3584]{1,0:T(8,128)(2,1)S(1)}, bf16[80,3584]{1,0:T(8,128)(2,1)S(1)}, u32[]{:S(2)}, u32[]{:S(2)}) %collective-permute-start.30) | collective-permute-done | bytes 573472 | tf_op jit(solution)/shard_map/cond/branch_1_fun/ppermute | solution.py:344
  233.3 5.9 %in_grads.5 = bf16[1,2,256,3584]{3,2,1,0:T(8,128)(2,1)} custom-call(bf16[320,512]{1,0:T(8,128)(2,1)} %copy-done.20, bf16[80,3584]{1,0:T(8,128)(2,1)} %copy-done.6, bf16[80,3584]{1,0:T(8,128)(2,1)} %copy-done.8, bf16[80,3584]{1,0:T(8,128)(2,1)} %copy-done.10, bf16[80,3584]{1,0:T(8,128)(2,1)} %copy-done.12), custom_call_target="tpu_custom_call" | custom-call | flops 1174405120 | bytes 5963776 | tf_op jit(solution)/shard_map/cond/branch_1_fun/in_grads/pallas_call | solution.py:255
  239.2 11.6 %adam.5 = (bf16[1,256,3584]{2,1,0:T(8,128)(2,1)}, f32[1,256,3584]{2,1,0:T(8,128)}, f32[1,256,3584]{2,1,0:T(8,128)}) custom-call(bf16[320,512]{1,0:T(8,128)(2,1)} %copy-done.20, bf16[3,256,3584]{2,1,0:T(8,128)(2,1)} %collective-permute-done.25.state_ref, bf16[80,3584]{1,0:T(8,128)(2,1)} %copy-done.6, bf16[80,3584]{1,0:T(8,128)(2,1)} %copy-done.8, ...), custom_call_target="tpu_custom_call" | custom-call | flops 587202560 | bytes 16973824 | tf_op jit(solution)/shard_map/cond/branch_1_fun/adam/pallas_call | solution.py:319
  (56 shorter events, 6.4 us)
Async XLA Ops:
  6.3 9.2 %copy-start.52 = (bf16[24,3584]{1,0:T(8,128)(2,1)S(1)}, bf16[24,3584]{1,0:T(8,128)(2,1)}, u32[]{:S(2)}) copy-start(bf16[24,3584]{1,0:T(8,128)(2,1)} %get-tuple-element.89) | copy-start | bytes 516100 | tf_op jit(solution)/shard_map/cond
  6.3 9.2 %copy-start.50 = (bf16[24,3584]{1,0:T(8,128)(2,1)S(1)}, bf16[24,3584]{1,0:T(8,128)(2,1)}, u32[]{:S(2)}) copy-start(bf16[24,3584]{1,0:T(8,128)(2,1)} %get-tuple-element.90) | copy-start | bytes 516100 | tf_op jit(solution)/shard_map/cond
  12.4 226.8 %collective-permute-start.25 = (bf16[3,256,3584]{2,1,0:T(8,128)(2,1)}, bf16[3,256,3584]{2,1,0:T(8,128)(2,1)}, u32[]{:S(2)}, u32[]{:S(2)}) collective-permute-start(bf16[3,256,3584]{2,1,0:T(8,128)(2,1)} %pack_state.5), channel_id=1, source_target_pairs={{16,0},{24,8},{8,16},{0,24},{17,1},{25,9},{9,17},{1,25},{18,2},{26... | collective-permute-start | bytes 16515080 | tf_op jit(solution)/shard_map/cond/branch_1_fun/ppermute | solution.py:389
  14.8 2.1 collective-permute-start.16
  15.5 123.3 %collective-permute-start.17 = (bf16[24,3584]{1,0:T(8,128)(2,1)S(1)}, bf16[24,3584]{1,0:T(8,128)(2,1)S(1)}, u32[]{:S(2)}, u32[]{:S(2)}) collective-permute-start(bf16[24,3584]{1,0:T(8,128)(2,1)S(1)} %copy-done.52), channel_id=1, source_target_pairs={{0,16},{8,24},{16,0},{24,8},{1,17},{9,25},{17,1},{25,9},{2,18},{10... | collective-permute-start | bytes 516104 | tf_op jit(solution)/shard_map/cond/branch_1_fun/ppermute | solution.py:388
  15.5 125.9 %collective-permute-start.18 = (bf16[24,3584]{1,0:T(8,128)(2,1)S(1)}, bf16[24,3584]{1,0:T(8,128)(2,1)S(1)}, u32[]{:S(2)}, u32[]{:S(2)}) collective-permute-start(bf16[24,3584]{1,0:T(8,128)(2,1)S(1)} %copy-done.50), channel_id=1, source_target_pairs={{0,24},{8,16},{16,8},{24,0},{1,25},{9,17},{17,9},{25,1},{2,26},{10... | collective-permute-start | bytes 516104 | tf_op jit(solution)/shard_map/cond/branch_1_fun/ppermute | solution.py:388
  16.9 124.5 %copy-start.42 = (bf16[24,3584]{1,0:T(8,128)(2,1)}, bf16[24,3584]{1,0:T(8,128)(2,1)S(1)}, u32[]{:S(2)}) copy-start(bf16[24,3584]{1,0:T(8,128)(2,1)S(1)} %collective-permute-done.16.refs_1_) | copy-start | bytes 516100 | tf_op jit(solution)/shard_map/cond
  144.4 28.8 %copy-start.36 = (bf16[40,3584]{1,0:T(8,128)(2,1)S(1)}, bf16[40,3584]{1,0:T(8,128)(2,1)}, u32[]{:S(2)}) copy-start(bf16[40,3584]{1,0:T(8,128)(2,1)} %get-tuple-element.98) | copy-start | bytes 860164 | tf_op jit(solution)/shard_map/cond
  144.4 28.7 %collective-permute-start.21 = (bf16[40,3584]{1,0:T(8,128)(2,1)}, bf16[40,3584]{1,0:T(8,128)(2,1)S(1)}, u32[]{:S(2)}, u32[]{:S(2)}) collective-permute-start(bf16[40,3584]{1,0:T(8,128)(2,1)} %get-tuple-element.91), channel_id=1, source_target_pairs={{0,6},{1,7},{2,4},{3,5},{4,2},{5,3},{6,0},{7,1},{8,14},{9,15},{10,... | collective-permute-start | bytes 860168 | tf_op jit(solution)/shard_map/cond/branch_1_fun/ppermute | solution.py:344
  148.0 25.0 %collective-permute-start.20 = (bf16[40,3584]{1,0:T(8,128)(2,1)}, bf16[40,3584]{1,0:T(8,128)(2,1)S(1)}, u32[]{:S(2)}, u32[]{:S(2)}) collective-permute-start(bf16[40,3584]{1,0:T(8,128)(2,1)} %get-tuple-element.91), channel_id=1, source_target_pairs={{0,4},{1,5},{2,6},{3,7},{4,0},{5,1},{6,2},{7,3},{8,12},{9,13},{10,... | collective-permute-start | bytes 860168 | tf_op jit(solution)/shard_map/cond/branch_1_fun/ppermute | solution.py:344
  148.0 25.1 %collective-permute-start.19 = (bf16[40,3584]{1,0:T(8,128)(2,1)}, bf16[40,3584]{1,0:T(8,128)(2,1)S(1)}, u32[]{:S(2)}, u32[]{:S(2)}) collective-permute-start(bf16[40,3584]{1,0:T(8,128)(2,1)} %get-tuple-element.91), channel_id=1, source_target_pairs={{0,2},{1,3},{2,0},{3,1},{4,6},{5,7},{6,4},{7,5},{8,10},{9,11},{10,... | collective-permute-start | bytes 860168 | tf_op jit(solution)/shard_map/cond/branch_1_fun/ppermute | solution.py:344
  173.1 28.1 %copy-start.24 = (bf16[80,3584]{1,0:T(8,128)(2,1)}, bf16[80,3584]{1,0:T(8,128)(2,1)S(1)}, u32[]{:S(2)}) copy-start(bf16[80,3584]{1,0:T(8,128)(2,1)S(1)} %constant_dynamic-update-slice_fusion.16.refs_1_) | copy-start | bytes 1720324 | tf_op jit(solution)/shard_map/cond
  173.1 27.4 %copy-start.22 = (bf16[80,3584]{1,0:T(8,128)(2,1)}, bf16[80,3584]{1,0:T(8,128)(2,1)S(1)}, u32[]{:S(2)}) copy-start(bf16[80,3584]{1,0:T(8,128)(2,1)S(1)} %constant_dynamic-update-slice_fusion.14.refs_0_) | copy-start | bytes 1720324 | tf_op jit(solution)/shard_map/cond
  173.2 27.4 %collective-permute-start.28 = (bf16[40,3584]{1,0:T(8,128)(2,1)S(1)}, bf16[40,3584]{1,0:T(8,128)(2,1)S(1)}, u32[]{:S(2)}, u32[]{:S(2)}) collective-permute-start(bf16[40,3584]{1,0:T(8,128)(2,1)S(1)} %copy-done.36), channel_id=1, source_target_pairs={{0,6},{1,7},{2,4},{3,5},{4,2},{5,3},{6,0},{7,1},{8,14},{9,15},{10,... | collective-permute-start | bytes 860168 | tf_op jit(solution)/shard_map/cond/branch_1_fun/ppermute | solution.py:344
  175.7 23.3 %collective-permute-start.27 = (bf16[40,3584]{1,0:T(8,128)(2,1)S(1)}, bf16[40,3584]{1,0:T(8,128)(2,1)S(1)}, u32[]{:S(2)}, u32[]{:S(2)}) collective-permute-start(bf16[40,3584]{1,0:T(8,128)(2,1)S(1)} %copy-done.36), channel_id=1, source_target_pairs={{0,4},{1,5},{2,6},{3,7},{4,0},{5,1},{6,2},{7,3},{8,12},{9,13},{10,... | collective-permute-start | bytes 860168 | tf_op jit(solution)/shard_map/cond/branch_1_fun/ppermute | solution.py:344
  175.7 18.0 %collective-permute-start.26 = (bf16[40,3584]{1,0:T(8,128)(2,1)S(1)}, bf16[40,3584]{1,0:T(8,128)(2,1)S(1)}, u32[]{:S(2)}, u32[]{:S(2)}) collective-permute-start(bf16[40,3584]{1,0:T(8,128)(2,1)S(1)} %copy-done.36), channel_id=1, source_target_pairs={{0,2},{1,3},{2,0},{3,1},{4,6},{5,7},{6,4},{7,5},{8,10},{9,11},{10,... | collective-permute-start | bytes 860168 | tf_op jit(solution)/shard_map/cond/branch_1_fun/ppermute | solution.py:344
  177.6 23.6 %collective-permute-start.22 = (bf16[80,3584]{1,0:T(8,128)(2,1)S(1)}, bf16[80,3584]{1,0:T(8,128)(2,1)S(1)}, u32[]{:S(2)}, u32[]{:S(2)}) collective-permute-start(bf16[80,3584]{1,0:T(8,128)(2,1)S(1)} %constant_dynamic-update-slice_fusion.14.refs_0_), channel_id=1, source_target_pairs={{0,1},{1,0},{2,3},{3,2},{4,5},{5,4},{6,7},{7,6},{8,9},{9,8},{10,11... | collective-permute-start | bytes 1720328 | tf_op jit(solution)/shard_map/cond/branch_1_fun/ppermute | solution.py:344
  193.7 15.9 %collective-permute-start.23 = (bf16[80,3584]{1,0:T(8,128)(2,1)S(1)}, bf16[80,3584]{1,0:T(8,128)(2,1)S(1)}, u32[]{:S(2)}, u32[]{:S(2)}) collective-permute-start(bf16[80,3584]{1,0:T(8,128)(2,1)S(1)} %constant_dynamic-update-slice_fusion.16.refs_1_), channel_id=1, source_target_pairs={{0,1},{1,0},{2,3},{3,2},{4,5},{5,4},{6,7},{7,6},{8,9},{9,8},{10,11... | collective-permute-start | bytes 1720328 | tf_op jit(solution)/shard_map/cond/branch_1_fun/ppermute | solution.py:344
  195.2 21.5 %copy-start.6 = (bf16[80,3584]{1,0:T(8,128)(2,1)}, bf16[80,3584]{1,0:T(8,128)(2,1)S(1)}, u32[]{:S(2)}) copy-start(bf16[80,3584]{1,0:T(8,128)(2,1)S(1)} %constant_dynamic-update-slice_fusion.18.refs_0_) | copy-start | bytes 1720324 | tf_op jit(solution)/shard_map/cond
  199.0 22.9 %collective-permute-start.29 = (bf16[80,3584]{1,0:T(8,128)(2,1)S(1)}, bf16[80,3584]{1,0:T(8,128)(2,1)S(1)}, u32[]{:S(2)}, u32[]{:S(2)}) collective-permute-start(bf16[80,3584]{1,0:T(8,128)(2,1)S(1)} %constant_dynamic-update-slice_fusion.18.refs_0_), channel_id=1, source_target_pairs={{0,1},{1,0},{2,3},{3,2},{4,5},{5,4},{6,7},{7,6},{8,9},{9,8},{10,11... | collective-permute-start | bytes 1720328 | tf_op jit(solution)/shard_map/cond/branch_1_fun/ppermute | solution.py:344
  200.6 16.2 %copy-start.8 = (bf16[80,3584]{1,0:T(8,128)(2,1)}, bf16[80,3584]{1,0:T(8,128)(2,1)S(1)}, u32[]{:S(2)}) copy-start(bf16[80,3584]{1,0:T(8,128)(2,1)S(1)} %constant_dynamic-update-slice_fusion.20.refs_1_) | copy-start | bytes 1720324 | tf_op jit(solution)/shard_map/cond
  200.6 31.1 %collective-permute-start.30 = (bf16[80,3584]{1,0:T(8,128)(2,1)S(1)}, bf16[80,3584]{1,0:T(8,128)(2,1)S(1)}, u32[]{:S(2)}, u32[]{:S(2)}) collective-permute-start(bf16[80,3584]{1,0:T(8,128)(2,1)S(1)} %constant_dynamic-update-slice_fusion.20.refs_1_), channel_id=1, source_target_pairs={{0,1},{1,0},{2,3},{3,2},{4,5},{5,4},{6,7},{7,6},{8,9},{9,8},{10,11... | collective-permute-start | bytes 1720328 | tf_op jit(solution)/shard_map/cond/branch_1_fun/ppermute | solution.py:344
  216.7 15.0 %collective-permute-start.24 = (bf16[320,512]{1,0:T(8,128)(2,1)}, bf16[320,512]{1,0:T(8,128)(2,1)S(1)}, u32[]{:S(2)}, u32[]{:S(2)}) collective-permute-start(bf16[320,512]{1,0:T(8,128)(2,1)} %factors.5), channel_id=1, source_target_pairs={{16,0},{24,8},{8,16},{0,24},{17,1},{25,9},{9,17},{1,25},{18,2},{26... | collective-permute-start | bytes 983048 | tf_op jit(solution)/shard_map/cond/branch_1_fun/ppermute | solution.py:397
  221.9 9.8 %copy-start.10 = (bf16[80,3584]{1,0:T(8,128)(2,1)}, bf16[80,3584]{1,0:T(8,128)(2,1)S(1)}, u32[]{:S(2)}) copy-start(bf16[80,3584]{1,0:T(8,128)(2,1)S(1)} %collective-permute-done.29.refs_2_) | copy-start | bytes 1720324 | tf_op jit(solution)/shard_map/cond
  (8 other events, 25.7 us)

commit v3 on v2

--- a/solution.py
+++ b/solution.py
@@ -168,8 +168,11 @@
     )(*arrays)
 
 
-def joined(refs):
-    return refs[0][...] if len(refs) == 1 else jnp.concatenate([ref[...] for ref in refs], axis=0)
+def rows_apart(refs, half):
+    blocks = [(ref, first) for ref in refs for first in range(0, ref.shape[0], 2 * half)]
+    token_rows = jnp.concatenate([ref[first : first + half] for ref, first in blocks], axis=0)
+    grad_rows = jnp.concatenate([ref[first + half : first + 2 * half] for ref, first in blocks], axis=0)
+    return token_rows, grad_rows
 
 
 def parts_spec(parts, tile):
@@ -179,33 +182,30 @@
 def factor_kernel(half, *refs):
     (w_in_ref, w_down_ref, out_ref, acc), x_refs = refs[-4:], refs[:-4]
     step = pl.program_id(0)
-    count, units = acc.shape[0], w_down_ref.shape[1]
+    units = w_down_ref.shape[1]
 
     @pl.when(step == 0)
     def _():
         acc[...] = jnp.zeros_like(acc)
 
-    x = joined(x_refs)
-    acc[:, 0:units] += dot(x, w_in_ref[0, 0], 1, 1)
-    acc[:, units : 2 * units] += dot(x, w_in_ref[0, 1], 1, 1)
-    acc[:, 2 * units : 3 * units] += dot(x, w_down_ref[0], 1, 1)
+    token_rows, grad_rows = rows_apart(x_refs, half)
+    acc[0] += dot(token_rows, w_in_ref[0, 0], 1, 1)
+    acc[1] += dot(token_rows, w_in_ref[0, 1], 1, 1)
+    acc[2] += dot(grad_rows, w_down_ref[0], 1, 1)
 
     @pl.when(step == pl.num_programs(0) - 1)
     def _():
-        gate = acc[:, 0:units]
-        up = acc[:, units : 2 * units]
-        back = pltpu.roll(acc[:, 2 * units : 3 * units], count - half, 0)
+        gate, up, back = acc[0], acc[1], acc[2]
         sig = jax.nn.sigmoid(gate)
         activated = gate * sig
         slopes = sig * (1.0 + gate * (1.0 - sig))
-        hidden = pltpu.roll(activated * up, half, 0)
-        is_token = lax.broadcasted_iota(jnp.int32, (count, units), 0) % (2 * half) < half
-        out_ref[:, 0:units] = jnp.where(is_token, back * up * slopes, hidden).astype(jnp.bfloat16)
-        out_ref[:, units : 2 * units] = jnp.where(is_token, back * activated, 0.0).astype(jnp.bfloat16)
+        out_ref[:, 0:units] = (back * up * slopes).astype(jnp.bfloat16)
+        out_ref[:, units : 2 * units] = (back * activated).astype(jnp.bfloat16)
+        out_ref[:, 2 * units : 3 * units] = (activated * up).astype(jnp.bfloat16)
 
 
 def factors_of(parts, w_in, w_down, half):
-    count, width = sum(part.shape[0] for part in parts), parts[0].shape[1]
+    count, width = sum(part.shape[0] for part in parts) // 2, parts[0].shape[1]
     units = w_down.shape[1]
     tile = tile_of(width, 896)
     return pl.pallas_call(
@@ -216,56 +216,13 @@
             pl.BlockSpec((1, 2, units, tile), lambda j: (0, 0, 0, j)),
             pl.BlockSpec((1, units, tile), lambda j: (0, 0, j)),
         ],
-        out_specs=pl.BlockSpec((count, 2 * units), lambda j: (0, 0)),
-        out_shape=jax.ShapeDtypeStruct((count, 2 * units), jnp.bfloat16),
-        scratch_shapes=[pltpu.VMEM((count, 3 * units), jnp.float32)],
+        out_specs=pl.BlockSpec((count, 3 * units), lambda j: (0, 0)),
+        out_shape=jax.ShapeDtypeStruct((count, 3 * units), jnp.bfloat16),
+        scratch_shapes=[pltpu.VMEM((3, count, units), jnp.float32)],
         compiler_params=params(),
-        cost_estimate=cost(6 * count * units * width, 6 * units * width + 2 * count * width),
+        cost_estimate=cost(6 * count * units * width, 6 * units * width + 4 * count * width),
         name="factors",
     )(*parts, w_in, w_down)
-
-
-def new_rows_of(crossing, x_refs):
-    if crossing is None:
-        return joined(x_refs)
-    own_slot = lax.axis_index("expert")
-    gathered = functools.reduce(jnp.logical_or, [own_slot == slot for slot in crossing])
-    return jnp.where(gathered, joined(x_refs[:-1]), x_refs[-1][...])
-
-
-def grad_kernel(half, crossing, factor_ref, *refs):
-    (out_ref, turned), x_refs = refs[-2:], refs[:-2]
-    units = out_ref.shape[2]
-
-    @pl.when(pl.program_id(0) == 0)
-    def _():
-        is_token = lax.broadcasted_iota(jnp.int32, factor_ref.shape, 0) % (2 * half) < half
-        both = factor_ref[...].astype(jnp.float32)
-        turned[...] = jnp.where(is_token, both, 0.0).T.astype(jnp.bfloat16)
-
-    grads = dot(turned[...], new_rows_of(crossing, x_refs), 1, 0)
-    out_ref[0, 0] = grads[:units].astype(jnp.bfloat16)
-    out_ref[0, 1] = grads[units:].astype(jnp.bfloat16)
-
-
-def grads_of(factors, crossing, parts, half):
-    count, width = factors.shape[0], parts[0].shape[1]
-    units = factors.shape[1] // 2
-    tile = tile_of(width, 896)
-    return pl.pallas_call(
-        functools.partial(grad_kernel, half, crossing),
-        grid=(width // tile,),
-        in_specs=[
-            pl.BlockSpec((count, 2 * units), lambda j: (0, 0)),
-            *parts_spec(parts, tile),
-        ],
-        out_specs=pl.BlockSpec((1, 2, units, tile), lambda j: (0, 0, 0, j)),
-        out_shape=jax.ShapeDtypeStruct((1, 2, units, width), jnp.bfloat16),
-        scratch_shapes=[pltpu.VMEM((2 * units, count), jnp.bfloat16)],
-        compiler_params=params(),
-        cost_estimate=cost(4 * count * units * width, 4 * units * width + 2 * count * width),
-        name="in_grads",
-    )(factors, *parts)
 
 
 def pack_kernel(*refs):
@@ -289,17 +246,25 @@
     )(*arrays)
 
 
-def adam_kernel(half, crossing, factor_ref, state_ref, *refs):
-    (down_ref, one_ref, two_ref, turned), x_refs = refs[-4:], refs[:-4]
-    count, units = factor_ref.shape[0], down_ref.shape[1]
+def finish_kernel(half, crossing, factor_ref, state_ref, *refs):
+    (down_ref, one_ref, two_ref, grad_ref, turned), x_refs = refs[-5:], refs[:-5]
+    units = down_ref.shape[1]
 
     @pl.when(pl.program_id(0) == 0)
     def _():
-        is_token = lax.broadcasted_iota(jnp.int32, (count, units), 0) % (2 * half) < half
-        both = factor_ref[:, :units].astype(jnp.float32)
-        turned[...] = jnp.where(is_token, 0.0, both).T.astype(jnp.bfloat16)
-
-    down_grad = dot(turned[...], new_rows_of(crossing, x_refs), 1, 0)
+        turned[...] = factor_ref[...].astype(jnp.float32).T.astype(jnp.bfloat16)
+
+    if crossing is None:
+        token_rows, grad_rows = rows_apart(x_refs, half)
+    else:
+        own_slot = lax.axis_index("expert")
+        gathered = functools.reduce(jnp.logical_or, [own_slot == slot for slot in crossing])
+        pairs = zip(rows_apart(x_refs[:-1], half), rows_apart(x_refs[-1:], half))
+        token_rows, grad_rows = [jnp.where(gathered, theirs, mine) for theirs, mine in pairs]
+    in_grads = dot(turned[: 2 * units], token_rows, 1, 0).astype(jnp.bfloat16)
+    grad_ref[0, 0] = in_grads[:units]
+    grad_ref[0, 1] = in_grads[units:]
+    down_grad = dot(turned[2 * units :], grad_rows, 1, 0)
     w_down, moment1, moment2 = [state_ref[k].astype(jnp.float32) for k in range(3)]
     rate = adam_rate / (1.0 - beta_one**adam_step)
     fix_two = 1.0 / (1.0 - beta_two**adam_step)
@@ -311,27 +276,27 @@
     two_ref[0] = second_new
 
 
-def adam(factors, crossing, parts, state, half):
+def finish(factors, crossing, parts, state, half):
     count = factors.shape[0]
     _, units, width = state.shape
     tile = tile_of(width, 512)
     spec = pl.BlockSpec((1, units, tile), lambda j: (0, 0, j))
+    kinds = (jnp.bfloat16, jnp.float32, jnp.float32)
     return pl.pallas_call(
-        functools.partial(adam_kernel, half, crossing),
+        functools.partial(finish_kernel, half, crossing),
         grid=(width // tile,),
         in_specs=[
-            pl.BlockSpec((count, 2 * units), lambda j: (0, 0)),
+            pl.BlockSpec((count, 3 * units), lambda j: (0, 0)),
             pl.BlockSpec((3, units, tile), lambda j: (0, 0, j)),
             *parts_spec(parts, tile),
         ],
-        out_specs=[spec, spec, spec],
-        out_shape=[
-            jax.ShapeDtypeStruct((1, units, width), kind) for kind in (jnp.bfloat16, jnp.float32, jnp.float32)
-        ],
-        scratch_shapes=[pltpu.VMEM((units, count), jnp.bfloat16)],
+        out_specs=[spec, spec, spec, pl.BlockSpec((1, 2, units, tile), lambda j: (0, 0, 0, j))],
+        out_shape=[jax.ShapeDtypeStruct((1, units, width), kind) for kind in kinds]
+        + [jax.ShapeDtypeStruct((1, 2, units, width), jnp.bfloat16)],
+        scratch_shapes=[pltpu.VMEM((3 * units, count), jnp.bfloat16)],
         compiler_params=params(),
-        cost_estimate=cost(2 * count * units * width, 16 * units * width + 2 * count * width),
-        name="adam",
+        cost_estimate=cost(6 * count * units * width, 20 * units * width + 4 * count * width),
+        name="finish",
     )(factors, state, *parts)
 
 
@@ -386,7 +351,7 @@
     for mask in range(1, expert_count):
         pairs = [(i, i ^ mask) for i in range(expert_count)]
         arrived.append(lax.ppermute(picked[mask], "expert", pairs))
-    state = move(pack(after(w_down, picked[0]), moment1, moment2))
+    state = move(after(pack(after(w_down, picked[0]), moment1, moment2), *arrived[1:]))
     own_block, new_block = join_pieces(arrived)
     own_parts = gather_dp(own_block, columns)
     factors = factors_of(own_parts, w_in, w_down, half)
@@ -395,8 +360,7 @@
         pairs = [(order[s], s) for s in range(expert_count) if s not in crossing]
         new_parts.append(lax.ppermute(jnp.concatenate(own_parts, axis=0), "expert", pairs))
     factors = move(factors)
-    grads = grads_of(factors, crossing, new_parts, half)
-    return (*adam(factors, crossing, new_parts, state, half), grads)
+    return tuple(finish(factors, crossing, new_parts, state, half))
 
 
 def local(tokens, grad_out, route_weights, expert_ids, swap_code, w_in, w_down, moment1, moment2):

time: 252 us -> 158 us (0.63)
  waiting for transfers between devices: 189 us -> 103 us
  Pallas kernels: 35.1 us -> 28.8 us
    ppermute x3, waiting for transfers between devices: 125 us -> 2.5 us  [layer(): arrived.append(lax.ppermute(picked[mask], 'expert', pairs))]
    ppermute x1, waiting for transfers between devices: 0.01 us -> 50.6 us  [layer(): factors = move(factors)]
    ppermute x10, waiting for transfers between devices: 65 us -> 50.1 us  [crossed(): return lax.ppermute(array, 'dp', [(i, i ^ mask) for i in range(size)])]
    pallas_call x2 -> x1, Pallas kernels: 17.5 us -> 11.9 us  [finish(): pl.pallas_call(functools.partial(finish_kernel, half, crossing), grid=(wi...]
  transfers between devices with their start and end apart: 15 -> 15, of which waited for: 8 -> 6; matrix products, arithmetic and copies ran while one was open for 0% -> 1% of each run, Pallas kernels for 6% -> 9%
where the time goes in v3:
time: 158 us; the launch traced here: 157 us
  waiting for transfers between devices  103 us (65%)
  Pallas kernels  28.8 us (18%)
  starting transfers between devices  18.6 us (12%)
  local copies, waits for them, and re-layouts  4.01 us (3%)
  between operations  2.11 us (1%)
    ppermute x1, waiting for transfers between devices, layer(): factors = move(factors)  50.6 us
    ppermute x10, waiting for transfers between devices, crossed(): return lax.ppermute(array, 'dp', [(i, i ^ mask) for i in range(size)])  50.1 us
    ppermute x10, starting transfers between devices, crossed(): return lax.ppermute(array, 'dp', [(i, i ^ mask) for i in range(size)])  13.9 us
    pallas_call x1, Pallas kernels, finish(): pl.pallas_call(functools.partial(finish_kernel, half, crossing), grid=(wi...  11.9 us
    pallas_call x1, Pallas kernels, pack(): pl.pallas_call(pack_kernel, grid=(width // tile,), in_specs=[pl.BlockSpec...  6.01 us
    pallas_call x1, Pallas kernels, factors_of(): pl.pallas_call(functools.partial(factor_kernel, half), grid=(width // til...  5.57 us
  transfers between devices with their start and end apart: 15, of which 6 were waited for; matrix products, arithmetic and copies ran while one was open for 1% of the time, Pallas kernels for 9%

profile of v3, /device:TPU:0, one launch (start us, length us, event | category | flops | bytes accessed | tf_op | source)
XLA Modules:
  0.0 157.3 jit_solution(18407566172441592469)
XLA Ops:
  0.6 1.3 fusion
  3.2 153.9 %conditional.1 = ((bf16[1,256,3584]{2,1,0:T(8,128)(2,1)}, f32[1,256,3584]{2,1,0:T(8,128)}, f32[1,256,3584]{2,1,0:T(8,128)}, bf16[1,2,256,3584]{3,2,1,0:T(8,128)(2,1)})) conditional(s32[]{:T(128)} %bitcast.8, (s32[128,8]{0,1:T(8,128)}, f32[128,8]{0,1:T(8,128)}, bf16[128,3584]{1,0:T(8,128)(2,1)}, ...), branch_computations={%region_0.0_spmd, %region_1.0_spmd, %region_2.0_spmd, %region_3.0_... | conditional | flops 1994653696 | bytes 134316992 | solution.py:386
  3.5 3.0 %pick_rows.7 = (bf16[24,3584]{1,0:T(8,128)(2,1)}, bf16[24,3584]{1,0:T(8,128)(2,1)}, bf16[24,3584]{1,0:T(8,128)(2,1)}, bf16[24,3584]{1,0:T(8,128)(2,1)}) custom-call(s32[8,128]{1,0:T(8,128)} %bitcast.12, f32[8,128]{1,0:T(8,128)} %bitcast.16, bf16[128,3584]{1,0:T(8,128)(2,1)} %get-tuple-element.117.refs_2_, bf16[128,3584]{1,0:T(8,128)(2,1)} %get-tuple-element.118.refs_3_), custom_call_target="tpu_custom_call" | custom-call | flops 176160768 | bytes 1835008 | tf_op jit(solution)/shard_map/cond/branch_3_fun/pick_rows/pallas_call | solution.py:108
  6.9 2.6 %collective-permute-start.48 = (bf16[24,3584]{1,0:T(8,128)(2,1)}, bf16[24,3584]{1,0:T(8,128)(2,1)S(1)}, u32[]{:S(2)}, u32[]{:S(2)}) collective-permute-start(bf16[24,3584]{1,0:T(8,128)(2,1)} %get-tuple-element.121), channel_id=1, source_target_pairs={{0,16},{8,24},{16,0},{24,8},{1,17},{9,25},{17,1},{25,9},{2,18},{10... | collective-permute-start | bytes 516104 | tf_op jit(solution)/shard_map/cond/branch_3_fun/ppermute | solution.py:353
  9.6 6.0 %pack_state.7 = bf16[3,256,3584]{2,1,0:T(8,128)(2,1)} custom-call(bf16[1,256,3584]{2,1,0:T(8,128)(2,1)S(1)} %copy-done.3, f32[1,256,3584]{2,1,0:T(8,128)} %get-tuple-element.127.refs_1_, f32[1,256,3584]{2,1,0:T(8,128)} %get-tuple-element.128.refs_2_), custom_call_target="tpu_custom_call" | custom-call | flops 1835008 | bytes 14680064 | tf_op jit(solution)/shard_map/cond/branch_3_fun/pack_state/pallas_call | solution.py:237
  15.6 2.5 %collective-permute-done.49.refs_3_ = bf16[24,3584]{1,0:T(8,128)(2,1)S(1)} collective-permute-done((bf16[24,3584]{1,0:T(8,128)(2,1)}, bf16[24,3584]{1,0:T(8,128)(2,1)S(1)}, u32[]{:S(2)}, u32[]{:S(2)}) %collective-permute-start.49) | collective-permute-done | bytes 172064 | tf_op jit(solution)/shard_map/cond/branch_3_fun/ppermute | solution.py:353
  18.1 1.4 collective-permute-start.56
  19.6 2.3 %join_pieces.7 = (bf16[40,3584]{1,0:T(8,128)(2,1)}, bf16[40,3584]{1,0:T(8,128)(2,1)}) custom-call(bf16[24,3584]{1,0:T(8,128)(2,1)} %get-tuple-element.119.refs_0_, bf16[24,3584]{1,0:T(8,128)(2,1)} %copy-done.37, bf16[24,3584]{1,0:T(8,128)(2,1)} %copy-done.41, bf16[24,3584]{1,0:T(8,128)(2,1)} %copy-done.45), custom_call_target="tpu_custom_call" | custom-call | flops 55050240 | bytes 1146880 | tf_op jit(solution)/shard_map/cond/branch_3_fun/join_pieces/pallas_call | solution.py:159
  21.8 3.6 %collective-permute-start.52 = (bf16[40,3584]{1,0:T(8,128)(2,1)}, bf16[40,3584]{1,0:T(8,128)(2,1)S(1)}, u32[]{:S(2)}, u32[]{:S(2)}) collective-permute-start(bf16[40,3584]{1,0:T(8,128)(2,1)} %get-tuple-element.123), channel_id=1, source_target_pairs={{0,6},{1,7},{2,4},{3,5},{4,2},{5,3},{6,0},{7,1},{8,14},{9,15},{10,... | collective-permute-start | bytes 860168 | tf_op jit(solution)/shard_map/cond/branch_3_fun/ppermute | solution.py:309
  25.5 0.8 collective-permute-start.50
  26.3 1.0 constant_dynamic-update-slice_fusion.37
  27.3 23.2 %collective-permute-done.51 = bf16[40,3584]{1,0:T(8,128)(2,1)S(1)} collective-permute-done((bf16[40,3584]{1,0:T(8,128)(2,1)}, bf16[40,3584]{1,0:T(8,128)(2,1)S(1)}, u32[]{:S(2)}, u32[]{:S(2)}) %collective-permute-start.51) | collective-permute-done | bytes 286752 | tf_op jit(solution)/shard_map/cond/branch_3_fun/ppermute | solution.py:309
  50.6 2.5 %collective-permute-start.59 = (bf16[40,3584]{1,0:T(8,128)(2,1)S(1)}, bf16[40,3584]{1,0:T(8,128)(2,1)S(1)}, u32[]{:S(2)}, u32[]{:S(2)}) collective-permute-start(bf16[40,3584]{1,0:T(8,128)(2,1)S(1)} %copy-done.29), channel_id=1, source_target_pairs={{0,6},{1,7},{2,4},{3,5},{4,2},{5,3},{6,0},{7,1},{8,14},{9,15},{10,... | collective-permute-start | bytes 860168 | tf_op jit(solution)/shard_map/cond/branch_3_fun/ppermute | solution.py:309
  53.2 1.9 %collective-permute-start.57 = (bf16[40,3584]{1,0:T(8,128)(2,1)S(1)}, bf16[40,3584]{1,0:T(8,128)(2,1)S(1)}, u32[]{:S(2)}, u32[]{:S(2)}) collective-permute-start(bf16[40,3584]{1,0:T(8,128)(2,1)S(1)} %copy-done.29), channel_id=1, source_target_pairs={{0,2},{1,3},{2,0},{3,1},{4,6},{5,7},{6,4},{7,5},{8,10},{9,11},{10,... | collective-permute-start | bytes 860168 | tf_op jit(solution)/shard_map/cond/branch_3_fun/ppermute | solution.py:309
  55.1 1.5 collective-permute-start.53
  56.6 14.6 %collective-permute-done.57 = bf16[40,3584]{1,0:T(8,128)(2,1)S(1)} collective-permute-done((bf16[40,3584]{1,0:T(8,128)(2,1)S(1)}, bf16[40,3584]{1,0:T(8,128)(2,1)S(1)}, u32[]{:S(2)}, u32[]{:S(2)}) %collective-permute-start.57) | collective-permute-done | bytes 286752 | tf_op jit(solution)/shard_map/cond/branch_3_fun/ppermute | solution.py:309
  71.2 1.5 collective-permute-start.54
  72.8 3.7 %collective-permute-done.58 = bf16[40,3584]{1,0:T(8,128)(2,1)S(1)} collective-permute-done((bf16[40,3584]{1,0:T(8,128)(2,1)S(1)}, bf16[40,3584]{1,0:T(8,128)(2,1)S(1)}, u32[]{:S(2)}, u32[]{:S(2)}) %collective-permute-start.58) | collective-permute-done | bytes 286752 | tf_op jit(solution)/shard_map/cond/branch_3_fun/ppermute | solution.py:309
  76.5 1.5 collective-permute-start.60
  78.7 8.5 %collective-permute-done.54.refs_3_ = bf16[80,3584]{1,0:T(8,128)(2,1)S(1)} collective-permute-done((bf16[80,3584]{1,0:T(8,128)(2,1)S(1)}, bf16[80,3584]{1,0:T(8,128)(2,1)S(1)}, u32[]{:S(2)}, u32[]{:S(2)}) %collective-permute-start.54) | collective-permute-done | bytes 573472 | tf_op jit(solution)/shard_map/cond/branch_3_fun/ppermute | solution.py:309
  87.2 0.8 copy-done.25
  88.0 5.6 %factors.7 = bf16[160,768]{1,0:T(8,128)(2,1)} custom-call(bf16[80,3584]{1,0:T(8,128)(2,1)} %copy-done.11, bf16[80,3584]{1,0:T(8,128)(2,1)} %copy-done.17, bf16[80,3584]{1,0:T(8,128)(2,1)} %copy-done.23, bf16[80,3584]{1,0:T(8,128)(2,1)} %copy-done.25, bf16[1,2,256,3584]{3,2,1,0:T(8,128)(2,1)} %get-tuple-element.124.refs_4_, bf16[1,256,3584]{2,1,0:T(8,128)(2,1)S(1)} %copy-done.3), custom_call_target="tpu_custom_call" | custom-call | flops 880803840 | bytes 7798784 | tf_op jit(solution)/shard_map/cond/branch_3_fun/factors/pallas_call | solution.py:211
  93.6 50.6 %collective-permute-done.55.factor_ref = bf16[160,768]{1,0:T(8,128)(2,1)S(1)} collective-permute-done((bf16[160,768]{1,0:T(8,128)(2,1)}, bf16[160,768]{1,0:T(8,128)(2,1)S(1)}, u32[]{:S(2)}, u32[]{:S(2)}) %collective-permute-start.55) | collective-permute-done | bytes 245792 | tf_op jit(solution)/shard_map/cond/branch_3_fun/ppermute | solution.py:362
  145.0 11.9 %finish.7 = (bf16[1,256,3584]{2,1,0:T(8,128)(2,1)}, f32[1,256,3584]{2,1,0:T(8,128)}, f32[1,256,3584]{2,1,0:T(8,128)}, bf16[1,2,256,3584]{3,2,1,0:T(8,128)(2,1)}) custom-call(bf16[160,768]{1,0:T(8,128)(2,1)} %copy-done.33, bf16[3,256,3584]{2,1,0:T(8,128)(2,1)} %collective-permute-done.56.state_ref, bf16[80,3584]{1,0:T(8,128)(2,1)} %copy-done.13, ...), custom_call_target="tpu_custom_call" | custom-call | flops 880803840 | bytes 20643840 | tf_op jit(solution)/shard_map/cond/branch_3_fun/finish/pallas_call | solution.py:285
  (45 shorter events, 2.1 us)
Async XLA Ops:
  3.5 6.1 %copy-start.3 = (bf16[1,256,3584]{2,1,0:T(8,128)(2,1)S(1)}, bf16[1,256,3584]{2,1,0:T(8,128)(2,1)}, u32[]{:S(2)}) copy-start(bf16[1,256,3584]{2,1,0:T(8,128)(2,1)} %get-tuple-element.126.refs_5_.refs_0_) | copy-start | bytes 5505028 | tf_op jit(solution)/shard_map/cond
  6.4 9.2 %collective-permute-start.47 = (bf16[24,3584]{1,0:T(8,128)(2,1)}, bf16[24,3584]{1,0:T(8,128)(2,1)S(1)}, u32[]{:S(2)}, u32[]{:S(2)}) collective-permute-start(bf16[24,3584]{1,0:T(8,128)(2,1)} %get-tuple-element.120), channel_id=1, source_target_pairs={{0,8},{8,0},{16,24},{24,16},{1,9},{9,1},{17,25},{25,17},{2,10},{10... | collective-permute-start | bytes 516104 | tf_op jit(solution)/shard_map/cond/branch_3_fun/ppermute | solution.py:353
  6.9 8.7 %collective-permute-start.48 = (bf16[24,3584]{1,0:T(8,128)(2,1)}, bf16[24,3584]{1,0:T(8,128)(2,1)S(1)}, u32[]{:S(2)}, u32[]{:S(2)}) collective-permute-start(bf16[24,3584]{1,0:T(8,128)(2,1)} %get-tuple-element.121), channel_id=1, source_target_pairs={{0,16},{8,24},{16,0},{24,8},{1,17},{9,25},{17,1},{25,9},{2,18},{10... | collective-permute-start | bytes 516104 | tf_op jit(solution)/shard_map/cond/branch_3_fun/ppermute | solution.py:353
  9.5 8.6 %collective-permute-start.49 = (bf16[24,3584]{1,0:T(8,128)(2,1)}, bf16[24,3584]{1,0:T(8,128)(2,1)S(1)}, u32[]{:S(2)}, u32[]{:S(2)}) collective-permute-start(bf16[24,3584]{1,0:T(8,128)(2,1)} %get-tuple-element.122), channel_id=1, source_target_pairs={{0,24},{8,16},{16,8},{24,0},{1,25},{9,17},{17,9},{25,1},{2,26},{10... | collective-permute-start | bytes 516104 | tf_op jit(solution)/shard_map/cond/branch_3_fun/ppermute | solution.py:353
  15.6 4.0 %copy-start.37 = (bf16[24,3584]{1,0:T(8,128)(2,1)}, bf16[24,3584]{1,0:T(8,128)(2,1)S(1)}, u32[]{:S(2)}) copy-start(bf16[24,3584]{1,0:T(8,128)(2,1)S(1)} %collective-permute-done.47.refs_1_) | copy-start | bytes 516100 | tf_op jit(solution)/shard_map/cond
  15.6 4.0 %copy-start.41 = (bf16[24,3584]{1,0:T(8,128)(2,1)}, bf16[24,3584]{1,0:T(8,128)(2,1)S(1)}, u32[]{:S(2)}) copy-start(bf16[24,3584]{1,0:T(8,128)(2,1)S(1)} %collective-permute-done.48.refs_2_) | copy-start | bytes 516100 | tf_op jit(solution)/shard_map/cond
  18.1 126.2 %collective-permute-start.56 = (bf16[3,256,3584]{2,1,0:T(8,128)(2,1)}, bf16[3,256,3584]{2,1,0:T(8,128)(2,1)}, u32[]{:S(2)}, u32[]{:S(2)}) collective-permute-start(bf16[3,256,3584]{2,1,0:T(8,128)(2,1)} %pack_state.7), channel_id=1, source_target_pairs={{24,0},{16,8},{8,16},{0,24},{25,1},{17,9},{9,17},{1,25},{26,2},{18... | collective-permute-start | bytes 16515080 | tf_op jit(solution)/shard_map/cond/branch_3_fun/ppermute | solution.py:354
  21.8 28.8 %copy-start.29 = (bf16[40,3584]{1,0:T(8,128)(2,1)S(1)}, bf16[40,3584]{1,0:T(8,128)(2,1)}, u32[]{:S(2)}) copy-start(bf16[40,3584]{1,0:T(8,128)(2,1)} %get-tuple-element.131) | copy-start | bytes 860164 | tf_op jit(solution)/shard_map/cond
  21.8 28.7 %collective-permute-start.52 = (bf16[40,3584]{1,0:T(8,128)(2,1)}, bf16[40,3584]{1,0:T(8,128)(2,1)S(1)}, u32[]{:S(2)}, u32[]{:S(2)}) collective-permute-start(bf16[40,3584]{1,0:T(8,128)(2,1)} %get-tuple-element.123), channel_id=1, source_target_pairs={{0,6},{1,7},{2,4},{3,5},{4,2},{5,3},{6,0},{7,1},{8,14},{9,15},{10,... | collective-permute-start | bytes 860168 | tf_op jit(solution)/shard_map/cond/branch_3_fun/ppermute | solution.py:309
  25.5 25.0 %collective-permute-start.51 = (bf16[40,3584]{1,0:T(8,128)(2,1)}, bf16[40,3584]{1,0:T(8,128)(2,1)S(1)}, u32[]{:S(2)}, u32[]{:S(2)}) collective-permute-start(bf16[40,3584]{1,0:T(8,128)(2,1)} %get-tuple-element.123), channel_id=1, source_target_pairs={{0,4},{1,5},{2,6},{3,7},{4,0},{5,1},{6,2},{7,3},{8,12},{9,13},{10,... | collective-permute-start | bytes 860168 | tf_op jit(solution)/shard_map/cond/branch_3_fun/ppermute | solution.py:309
  25.5 25.1 %collective-permute-start.50 = (bf16[40,3584]{1,0:T(8,128)(2,1)}, bf16[40,3584]{1,0:T(8,128)(2,1)S(1)}, u32[]{:S(2)}, u32[]{:S(2)}) collective-permute-start(bf16[40,3584]{1,0:T(8,128)(2,1)} %get-tuple-element.123), channel_id=1, source_target_pairs={{0,2},{1,3},{2,0},{3,1},{4,6},{5,7},{6,4},{7,5},{8,10},{9,11},{10,... | collective-permute-start | bytes 860168 | tf_op jit(solution)/shard_map/cond/branch_3_fun/ppermute | solution.py:309
  50.6 37.4 %copy-start.17 = (bf16[80,3584]{1,0:T(8,128)(2,1)}, bf16[80,3584]{1,0:T(8,128)(2,1)S(1)}, u32[]{:S(2)}) copy-start(bf16[80,3584]{1,0:T(8,128)(2,1)S(1)} %constant_dynamic-update-slice_fusion.38.refs_1_) | copy-start | bytes 1720324 | tf_op jit(solution)/shard_map/cond
  50.6 37.3 %copy-start.11 = (bf16[80,3584]{1,0:T(8,128)(2,1)}, bf16[80,3584]{1,0:T(8,128)(2,1)S(1)}, u32[]{:S(2)}) copy-start(bf16[80,3584]{1,0:T(8,128)(2,1)S(1)} %constant_dynamic-update-slice_fusion.36.refs_0_) | copy-start | bytes 1720324 | tf_op jit(solution)/shard_map/cond
  50.6 27.4 %collective-permute-start.59 = (bf16[40,3584]{1,0:T(8,128)(2,1)S(1)}, bf16[40,3584]{1,0:T(8,128)(2,1)S(1)}, u32[]{:S(2)}, u32[]{:S(2)}) collective-permute-start(bf16[40,3584]{1,0:T(8,128)(2,1)S(1)} %copy-done.29), channel_id=1, source_target_pairs={{0,6},{1,7},{2,4},{3,5},{4,2},{5,3},{6,0},{7,1},{8,14},{9,15},{10,... | collective-permute-start | bytes 860168 | tf_op jit(solution)/shard_map/cond/branch_3_fun/ppermute | solution.py:309
  53.2 23.3 %collective-permute-start.58 = (bf16[40,3584]{1,0:T(8,128)(2,1)S(1)}, bf16[40,3584]{1,0:T(8,128)(2,1)S(1)}, u32[]{:S(2)}, u32[]{:S(2)}) collective-permute-start(bf16[40,3584]{1,0:T(8,128)(2,1)S(1)} %copy-done.29), channel_id=1, source_target_pairs={{0,4},{1,5},{2,6},{3,7},{4,0},{5,1},{6,2},{7,3},{8,12},{9,13},{10,... | collective-permute-start | bytes 860168 | tf_op jit(solution)/shard_map/cond/branch_3_fun/ppermute | solution.py:309
  53.2 18.0 %collective-permute-start.57 = (bf16[40,3584]{1,0:T(8,128)(2,1)S(1)}, bf16[40,3584]{1,0:T(8,128)(2,1)S(1)}, u32[]{:S(2)}, u32[]{:S(2)}) collective-permute-start(bf16[40,3584]{1,0:T(8,128)(2,1)S(1)} %copy-done.29), channel_id=1, source_target_pairs={{0,2},{1,3},{2,0},{3,1},{4,6},{5,7},{6,4},{7,5},{8,10},{9,11},{10,... | collective-permute-start | bytes 860168 | tf_op jit(solution)/shard_map/cond/branch_3_fun/ppermute | solution.py:309
  55.1 23.6 %collective-permute-start.53 = (bf16[80,3584]{1,0:T(8,128)(2,1)S(1)}, bf16[80,3584]{1,0:T(8,128)(2,1)S(1)}, u32[]{:S(2)}, u32[]{:S(2)}) collective-permute-start(bf16[80,3584]{1,0:T(8,128)(2,1)S(1)} %constant_dynamic-update-slice_fusion.36.refs_0_), channel_id=1, source_target_pairs={{0,1},{1,0},{2,3},{3,2},{4,5},{5,4},{6,7},{7,6},{8,9},{9,8},{10,11... | collective-permute-start | bytes 1720328 | tf_op jit(solution)/shard_map/cond/branch_3_fun/ppermute | solution.py:309
  71.2 15.9 %collective-permute-start.54 = (bf16[80,3584]{1,0:T(8,128)(2,1)S(1)}, bf16[80,3584]{1,0:T(8,128)(2,1)S(1)}, u32[]{:S(2)}, u32[]{:S(2)}) collective-permute-start(bf16[80,3584]{1,0:T(8,128)(2,1)S(1)} %constant_dynamic-update-slice_fusion.38.refs_1_), channel_id=1, source_target_pairs={{0,1},{1,0},{2,3},{3,2},{4,5},{5,4},{6,7},{7,6},{8,9},{9,8},{10,11... | collective-permute-start | bytes 1720328 | tf_op jit(solution)/shard_map/cond/branch_3_fun/ppermute | solution.py:309
  72.7 20.8 %copy-start.13 = (bf16[80,3584]{1,0:T(8,128)(2,1)}, bf16[80,3584]{1,0:T(8,128)(2,1)S(1)}, u32[]{:S(2)}) copy-start(bf16[80,3584]{1,0:T(8,128)(2,1)S(1)} %constant_dynamic-update-slice_fusion.40.refs_0_) | copy-start | bytes 1720324 | tf_op jit(solution)/shard_map/cond
  76.5 67.8 %collective-permute-start.60 = (bf16[80,3584]{1,0:T(8,128)(2,1)S(1)}, bf16[80,3584]{1,0:T(8,128)(2,1)}, u32[]{:S(2)}, u32[]{:S(2)}) collective-permute-start(bf16[80,3584]{1,0:T(8,128)(2,1)S(1)} %constant_dynamic-update-slice_fusion.40.refs_0_), channel_id=1, source_target_pairs={{0,1},{1,0},{2,3},{3,2},{4,5},{5,4},{6,7},{7,6},{8,9},{9,8},{10,11... | collective-permute-start | bytes 1720328 | tf_op jit(solution)/shard_map/cond/branch_3_fun/ppermute | solution.py:309
  78.0 15.5 %copy-start.15 = (bf16[80,3584]{1,0:T(8,128)(2,1)}, bf16[80,3584]{1,0:T(8,128)(2,1)S(1)}, u32[]{:S(2)}) copy-start(bf16[80,3584]{1,0:T(8,128)(2,1)S(1)} %constant_dynamic-update-slice_fusion.42.refs_1_) | copy-start | bytes 1720324 | tf_op jit(solution)/shard_map/cond
  78.1 66.2 %collective-permute-start.61 = (bf16[80,3584]{1,0:T(8,128)(2,1)S(1)}, bf16[80,3584]{1,0:T(8,128)(2,1)}, u32[]{:S(2)}, u32[]{:S(2)}) collective-permute-start(bf16[80,3584]{1,0:T(8,128)(2,1)S(1)} %constant_dynamic-update-slice_fusion.42.refs_1_), channel_id=1, source_target_pairs={{0,1},{1,0},{2,3},{3,2},{4,5},{5,4},{6,7},{7,6},{8,9},{9,8},{10,11... | collective-permute-start | bytes 1720328 | tf_op jit(solution)/shard_map/cond/branch_3_fun/ppermute | solution.py:309
  78.7 8.5 %copy-start.23 = (bf16[80,3584]{1,0:T(8,128)(2,1)}, bf16[80,3584]{1,0:T(8,128)(2,1)S(1)}, u32[]{:S(2)}) copy-start(bf16[80,3584]{1,0:T(8,128)(2,1)S(1)} %collective-permute-done.53.refs_2_) | copy-start | bytes 1720324 | tf_op jit(solution)/shard_map/cond
  93.5 50.7 %collective-permute-start.55 = (bf16[160,768]{1,0:T(8,128)(2,1)}, bf16[160,768]{1,0:T(8,128)(2,1)S(1)}, u32[]{:S(2)}, u32[]{:S(2)}) collective-permute-start(bf16[160,768]{1,0:T(8,128)(2,1)} %factors.7), channel_id=1, source_target_pairs={{24,0},{16,8},{8,16},{0,24},{25,1},{17,9},{9,17},{1,25},{26,2},{18... | collective-permute-start | bytes 737288 | tf_op jit(solution)/shard_map/cond/branch_3_fun/ppermute | solution.py:362
  (3 other events, 3.0 us)
